TPU v7x, 128 devices: a whole 4x4x4 slice. The times are simulated.
128 devices in a mesh: leaf: 32 (over y, x, core), blk: 4 (over z).
Axes of the slice: x: 4, y: 4, z: 4, core: 2. Of those that a mesh axis runs over, the one named last changes fastest.
Arguments:
- leaf_basis: float32 [2048, 64, 64], P(('leaf', 'blk')), may hold values from -5.5 to 6.5
- leaf_transfer: float32 [2048, 64, 64], P(('leaf', 'blk')), may hold values from -0.5 to 1
- inner_transfer: float32 [2016, 64, 64], P('leaf'), may hold values from -0.5 to 1
- upper_transfer: float32 [31, 64, 64], replicated, may hold values from -0.5 to 1
- coupling: float32 [32768, 64, 64], P(('leaf', 'blk')), may hold values from -6 to 6
- pairs: int32 [32768, 2], P(('leaf', 'blk')), may hold values from 0 to 2047, as said below
- counts: int32 [128], P(('leaf', 'blk')), may hold values from 64 to 256, as said below
Outputs:
- leaf_orth: float32 [2048, 64, 64], P(('leaf', 'blk'))
- new_leaf_transfer: float32 [2048, 64, 64], P(('leaf', 'blk'))
- new_inner_transfer: float32 [2016, 64, 64], P('leaf')
- new_upper: float32 [32, 64, 64], P('leaf')
- reprojected: float32 [32768, 64, 64], P(('leaf', 'blk'))
Inputs may be any that keep to these rules, and one draw needn't show every extreme that they name: `pairs`: slots of leaf index d have a row cluster in [d * 64, (d + 1) * 64) and a column cluster in [(d - 1) * 64, (d + 2) * 64). `counts`: the live slots of a device are its leading ones; some device has all 256 live.
All inputs are finite; a program needn't handle non-finite values.
Results may differ from a plain program's by a relative error of at most 0.0003.
Values sent between devices are 32-bit elements; how exact they have to be, the bound alone decides.
A program may use at most 128 MiB of HBM per device.

v0:
```python
import jax
import jax.numpy as jnp
from jax import lax
from jax.sharding import PartitionSpec as P

highest = lax.Precision.HIGHEST


def extended(cells, sides, width):
    for axis, dim in sides:
        count = lax.axis_size(axis)
        ends = count - 1
        head = lax.slice_in_dim(cells, 0, width, axis=dim)
        tail = lax.slice_in_dim(cells, cells.shape[dim] - width, cells.shape[dim], axis=dim)
        cells = jnp.concatenate(
            [
                lax.ppermute(tail, axis, [(i, (i + 1) % count) for i in range(ends)]),
                cells,
                lax.ppermute(head, axis, [((i + 1) % count, i) for i in range(ends)]),
            ],
            axis=dim,
        )
    return cells


def swapped(value, axis, bit):
    return lax.ppermute(value, axis, [(i, i ^ 1 << bit) for i in range(lax.axis_size(axis))])


def times_right(left, right):
    return jnp.einsum("...ab,...bc->...ac", left, right, precision=highest)


def transpose_times(left, right):
    return jnp.einsum("...ba,...bc->...ac", left, right, precision=highest)


def flipped(matrix):
    return jnp.swapaxes(matrix, -1, -2)


def sandwich(transfer, gram):
    return transpose_times(transfer, times_right(gram, transfer))


def retransfer(child_factor, transfer, parent_factor):
    carried = transpose_times(child_factor, transfer)
    solved = lax.linalg.triangular_solve(
        parent_factor, flipped(carried), left_side=True, lower=True
    )
    return flipped(solved)


def body(leaf_basis, leaf_transfer, inner_transfer, upper_transfer, coupling, pairs, counts):
    quarter = leaf_basis.shape[0]
    blk_count = lax.axis_size("blk")
    group = quarter * blk_count
    nleaf = lax.axis_size("leaf")
    leaf_pos = lax.axis_index("leaf")
    blk_pos = lax.axis_index("blk")
    leaf_gram = transpose_times(leaf_basis, leaf_basis)
    factor = jnp.linalg.cholesky(leaf_gram)
    leaf_orth = flipped(
        lax.linalg.triangular_solve(factor, flipped(leaf_basis), left_side=True, lower=True)
    )
    leaf_images = sandwich(leaf_transfer, leaf_gram)
    all_factor, all_images = (
        lax.all_gather(factor, "blk", axis=0, tiled=True),
        lax.all_gather(leaf_images, "blk", axis=0, tiled=True),
    )
    nearby = extended(all_factor, (("leaf", 0),), group)
    levels = group.bit_length() - 1
    images = all_images
    child_factor = None
    child_transfer = None
    inner_parts = []
    new_leaf = None
    for level in range(levels - 1, -1, -1):
        node_gram = images[0::2] + images[1::2]
        node_factor = jnp.linalg.cholesky(node_gram)
        if child_factor is None:
            parents = lax.dynamic_slice_in_dim(
                node_factor, blk_pos * (quarter // 2), quarter // 2, 0
            )
            new_leaf = retransfer(factor, leaf_transfer, jnp.repeat(parents, 2, axis=0))
        else:
            inner_parts.insert(
                0, retransfer(child_factor, child_transfer, jnp.repeat(node_factor, 2, axis=0))
            )
        node_transfer = inner_transfer[2**level - 1 : 2 ** (level + 1) - 1]
        images = sandwich(node_transfer, node_gram)
        child_factor = node_factor
        child_transfer = node_transfer
    upward = nleaf.bit_length() - 1
    chain_factor = [child_factor[0]]
    chain_transfer = [child_transfer[0]]
    mine = images[0]
    for level in range(1, upward + 1):
        partner = swapped(mine, "leaf", level - 1)
        node_gram = mine + partner
        node_factor = jnp.linalg.cholesky(node_gram)
        owner_entry = (leaf_pos >> level << level) + 2 ** (level - 1) - 1
        node_transfer = lax.dynamic_index_in_dim(upper_transfer, owner_entry, 0, keepdims=False)
        chain_factor.append(node_factor)
        chain_transfer.append(node_transfer)
        if level < upward:
            mine = sandwich(node_transfer, node_gram)
    root_renewed = retransfer(chain_factor[0], chain_transfer[0], chain_factor[1])
    new_inner = jnp.concatenate([root_renewed[None]] + inner_parts, axis=0)
    upper_out = flipped(chain_factor[upward])
    top_carried = transpose_times(chain_factor[upward], chain_transfer[upward])
    upper_out = jnp.where(leaf_pos == 2 ** (upward - 1), top_carried, upper_out)
    for level in range(1, upward):
        renewed = retransfer(chain_factor[level], chain_transfer[level], chain_factor[level + 1])
        upper_out = jnp.where(leaf_pos % 2**level == 2 ** (level - 1), renewed, upper_out)
    new_upper = upper_out[None]
    row_local = pairs[:, 0] - leaf_pos * group
    col_local = pairs[:, 1] - (leaf_pos - 1) * group
    row_factor = all_factor[row_local]
    col_factor = nearby[col_local]
    result = transpose_times(row_factor, times_right(coupling, col_factor))
    live = jnp.arange(coupling.shape[0], dtype=jnp.int32) < counts[0]
    reprojected = jnp.where(live[:, None, None], result, jnp.float32(0.0))
    return (leaf_orth, new_leaf, new_inner, new_upper, reprojected)


def solution(mesh):
    in_specs = (
        P(("leaf", "blk"), None, None),
        P(("leaf", "blk"), None, None),
        P("leaf", None, None),
        P(),
        P(("leaf", "blk"), None, None),
        P(("leaf", "blk"), None),
        P(("leaf", "blk")),
    )
    out_specs = (
        P(("leaf", "blk"), None, None),
        P(("leaf", "blk"), None, None),
        P("leaf", None, None),
        P("leaf", None, None),
        P(("leaf", "blk"), None, None),
    )
    return jax.shard_map(body, mesh=mesh, in_specs=in_specs, out_specs=out_specs, check_vma=False)
```

profile of v0, /device:TPU:1, one launch (start us, length us, event | category | flops | bytes accessed | tf_op | source)
XLA Modules:
  0.0 1144.1 jit_solution(6332645935317991121)
XLA Ops:
  13.7 94.6 %custom-call.59 = f32[16,64,64]{2,1,0:T(8,128)} custom-call(f32[16,64,64]{2,1,0:T(8,128)S(1)} %fusion.16), custom_call_target="Cholesky" | custom-call | tf_op jit(solution)/shard_map/jit(cholesky)/cholesky | solution.py:62
  108.3 9.2 copy.206
  153.0 189.3 %custom-call.43 = f32[32,64,64]{2,1,0:T(8,128)} custom-call(f32[32,64,64]{2,1,0:T(8,128)} %fusion.5), custom_call_target="Cholesky" | custom-call | tf_op jit(solution)/shard_map/jit(cholesky)/cholesky | solution.py:80
  345.6 48.3 %custom-call.49 = f32[8,64,64]{2,1,0:T(8,128)} custom-call(f32[8,64,64]{2,1,0:T(8,128)} %fusion.22), custom_call_target="Cholesky" | custom-call | tf_op jit(solution)/shard_map/jit(cholesky)/cholesky | solution.py:80
  397.2 95.2 %custom-call.63 = f32[16,64,64]{2,1,0:T(8,128)} custom-call(f32[16,64,64]{2,1,0:T(8,128)} %fusion.11), custom_call_target="Cholesky" | custom-call | tf_op jit(solution)/shard_map/jit(cholesky)/cholesky | solution.py:80
  509.0 80.4 %custom-call.64 = f32[16,1,64,64]{2,3,1,0:T(8,128)} custom-call(f32[16,1,64,64]{3,2,1,0:T(8,128)} %bitcast.248), custom_call_target="InvertDiagBlocksLowerTriangular" | custom-call | tf_op jit(solution)/shard_map/triangular_solve/custom-call.7 | solution.py:48
  590.7 6.6 custom-call.44
  600.8 12.5 %custom-call.45 = f32[2,64,64]{2,1,0:T(8,128)S(1)} custom-call(f32[2,64,64]{2,1,0:T(8,128)} %fusion.36), custom_call_target="Cholesky" | custom-call | tf_op jit(solution)/shard_map/jit(cholesky)/cholesky | solution.py:80
  616.1 24.2 %custom-call.47 = f32[4,64,64]{2,1,0:T(8,128)S(1)} custom-call(f32[4,64,64]{2,1,0:T(8,128)} %fusion.29), custom_call_target="Cholesky" | custom-call | tf_op jit(solution)/shard_map/jit(cholesky)/cholesky | solution.py:80
  648.9 80.0 %custom-call.61 = f32[16,1,64,64]{2,3,1,0:T(8,128)} custom-call(f32[16,1,64,64]{3,2,1,0:T(8,128)} %bitcast.247), custom_call_target="InvertDiagBlocksLowerTriangular" | custom-call | tf_op jit(solution)/shard_map/triangular_solve/custom-call.7 | solution.py:48
  728.9 80.0 %custom-call.60 = f32[16,1,64,64]{2,3,1,0:T(8,128)} custom-call(f32[16,1,64,64]{3,2,1,0:T(8,128)} %get-tuple-element.38), custom_call_target="InvertDiagBlocksLowerTriangular" | custom-call | tf_op jit(solution)/shard_map/triangular_solve/custom-call.7 | solution.py:64
  819.9 11.2 custom-call.46
  831.1 20.3 %custom-call.48 = f32[4,1,64,64]{2,3,1,0:T(8,128)} custom-call(f32[4,1,64,64]{3,2,1,0:T(8,128)S(1)} %broadcast_select_fusion.3), custom_call_target="InvertDiagBlocksLowerTriangular" | custom-call | tf_op jit(solution)/shard_map/triangular_solve | solution.py:48
  851.3 40.1 %custom-call.50 = f32[8,1,64,64]{2,3,1,0:T(8,128)} custom-call(f32[8,1,64,64]{3,2,1,0:T(8,128)S(1)} %broadcast_select_fusion.2), custom_call_target="InvertDiagBlocksLowerTriangular" | custom-call | tf_op jit(solution)/shard_map/triangular_solve | solution.py:48
  891.4 68.5 %custom-call.51 = f32[32,1,64,64]{0,2,3,1:T(8,128)} custom-call(f32[32,1,64,64]{0,3,2,1:T(8,128)} %broadcast_select_fusion.1), custom_call_target="InvertDiagBlocksLowerTriangular" | custom-call | tf_op jit(solution)/shard_map/triangular_solve | solution.py:48
  971.3 6.6 cholesky.323
  980.0 6.3 custom-call.62
  1016.0 5.8 cholesky.367
  1069.7 6.2 gather_fusion
  1080.0 6.0 pad_maximum_fusion
  1086.0 7.2 gather_fusion.1
  1093.2 17.6 %fusion.140 = f32[256,64,64]{2,1,0:T(8,128)S(1)} fusion(f32[256,64,64]{2,1,0:T(8,128)} %gather_fusion.1, f32[256,64,64]{2,1,0:T(8,128)} %copy.206), kind=kOutput, calls=%fused_computation.244 | convolution fusion | flops 805306368 | bytes 12582912 | tf_op jit(solution)/shard_map/...ab,...bc->...ac/dot_general | solution.py:31
  1110.8 18.3 %broadcast_select_fusion = f32[256,64,64]{2,1,0:T(8,128)} fusion(pred[256]{0:T(512)(128)(4,1)S(1)} %copy-done.25, f32[256,64,64]{2,1,0:T(8,128)} %gather_fusion, f32[256,64,64]{2,1,0:T(8,128)S(1)} %fusion.140), kind=kOutput, calls=%fused_computation.3 | convolution fusion | flops 806354944 | bytes 12583168 | tf_op jit(solution)/shard_map/...ba,...bc->...ac/dot_general | solution.py:35
  1129.1 7.8 copy.211
  (219 shorter events, 186.0 us)
Async XLA Ops:
  7.2 960.4 %copy-start = (f32[31,64,64]{2,1,0:T(8,128)S(1)}, f32[31,64,64]{2,1,0:T(8,128)}, u32[]{:S(2)}) copy-start(f32[31,64,64]{2,1,0:T(8,128)} %param.16) | copy-start | bytes 1523716
  7.2 4.4 copy-start.5
  7.2 112.2 %all-gather.3.cloned.1.call-start = ((), (), s32[]{:S(2)}) async-start(), calls=%async_computation | async-start | bytes 2621440 | tf_op jit(solution)/shard_map/all_gather | solution.py:69
  13.3 1034.1 %all-gather.5.cloned.1.call-start = ((), (), s32[]{:S(2)}) async-start(), calls=%async_computation.1 | async-start | bytes 2621440 | tf_op jit(solution)/shard_map/all_gather | solution.py:68
  108.3 10.5 copy-start.23
  123.7 5.4 copy-start.3
  500.1 89.3 %copy-start.19 = (f32[2,64,64]{1,2,0:T(8,128)S(1)}, f32[2,64,64]{1,2,0:T(8,128)}, u32[]{:S(2)}) copy-start(f32[2,64,64]{1,2,0:T(8,128)} %copy-done.18) | copy-start | bytes 98308
  500.1 99.3 %copy-start.15 = (f32[4,64,64]{1,2,0:T(8,128)S(1)}, f32[4,64,64]{1,2,0:T(8,128)}, u32[]{:S(2)}) copy-start(f32[4,64,64]{1,2,0:T(8,128)} %copy-done.14) | copy-start | bytes 196612
  504.7 461.3 %collective-permute-start = (f32[64,64]{0,1:T(8,128)}, f32[64,64]{0,1:T(8,128)}, u32[]{:S(2)}, u32[]{:S(2)}) collective-permute-start(f32[64,64]{0,1:T(8,128)} %convolution_bitcast_fusion.17), channel_id=1, source_target_pairs={{0,4},{4,0},{8,12},{12,8},{16,20},{20,16},{24,28},{28,24},{32,36},... | collective-permute-start | bytes 49160 | tf_op jit(solution)/shard_map/ppermute | solution.py:27
  808.9 6.1 copy-start.10
  808.9 6.1 copy-start.20
  817.8 145.1 %copy-start.13 = (f32[16,64,64]{1,2,0:T(8,128)S(1)}, f32[16,64,64]{1,2,0:T(8,128)}, u32[]{:S(2)}) copy-start(f32[16,64,64]{1,2,0:T(8,128)} %convolution_bitcast_fusion.4) | copy-start | bytes 786436
  962.9 28.2 %copy-start.21 = (f32[4,64,64]{2,1,0:T(8,128)S(1)}, f32[4,64,64]{2,1,0:T(8,128)}, u32[]{:S(2)}) copy-start(f32[4,64,64]{2,1,0:T(8,128)} %fusion.30) | copy-start | bytes 196612
  962.9 29.4 %copy-start.16 = (f32[8,64,64]{2,1,0:T(8,128)S(1)}, f32[8,64,64]{2,1,0:T(8,128)}, u32[]{:S(2)}) copy-start(f32[8,64,64]{2,1,0:T(8,128)} %fusion.23) | copy-start | bytes 393220
  963.9 30.8 %copy-start.9 = (f32[32,64,64]{2,1,0:T(8,128)S(1)}, f32[32,64,64]{2,1,0:T(8,128)}, u32[]{:S(2)}) copy-start(f32[32,64,64]{2,1,0:T(8,128)} %fusion.6) | copy-start | bytes 1572868
  968.6 28.9 %collective-permute-start.1 = (f32[64,64]{0,1:T(8,128)}, f32[64,64]{0,1:T(8,128)}, u32[]{:S(2)}, u32[]{:S(2)}) collective-permute-start(f32[64,64]{0,1:T(8,128)} %fusion.53), channel_id=1, source_target_pairs={{0,8},{4,12},{8,0},{12,4},{16,24},{20,28},{24,16},{28,20},{32,40},... | collective-permute-start | bytes 49160 | tf_op jit(solution)/shard_map/ppermute | solution.py:27
  1011.3 4.6 collective-permute-start.2
  1028.6 2.8 collective-permute-start.3
  1044.1 11.6 %collective-permute-start.4 = (f32[64,64]{0,1:T(8,128)S(1)}, f32[64,64]{0,1:T(8,128)S(1)}, u32[]{:S(2)}, u32[]{:S(2)}) collective-permute-start(f32[64,64]{0,1:T(8,128)S(1)} %fusion.71), channel_id=1, source_target_pairs={{0,64},{4,68},{8,72},{12,76},{16,80},{20,84},{24,88},{28,92},{32,9... | collective-permute-start | bytes 49160 | tf_op jit(solution)/shard_map/ppermute | solution.py:27
  1047.4 28.5 %collective-permute-start.5 = (f32[64,64,64]{2,1,0:T(8,128)}, f32[64,64,64]{2,1,0:T(8,128)}, u32[]{:S(2)}, u32[]{:S(2)}) collective-permute-start(f32[64,64,64]{2,1,0:T(8,128)} %all-gather.5.cloned.1.call-done), channel_id=1, source_target_pairs={{0,4},{4,8},{8,12},{12,16},{16,20},{20,24},{24,28},{28,32},{32,36}... | collective-permute-start | bytes 3145736 | tf_op jit(solution)/shard_map/ppermute | solution.py:17
  1052.3 27.7 %collective-permute-start.6 = (f32[64,64,64]{2,1,0:T(8,128)}, f32[64,64,64]{2,1,0:T(8,128)}, u32[]{:S(2)}, u32[]{:S(2)}) collective-permute-start(f32[64,64,64]{2,1,0:T(8,128)} %all-gather.5.cloned.1.call-done), channel_id=1, source_target_pairs={{4,0},{8,4},{12,8},{16,12},{20,16},{24,20},{28,24},{32,28},{36,32}... | collective-permute-start | bytes 3145736 | tf_op jit(solution)/shard_map/ppermute | solution.py:19
  1069.7 10.2 copy-start.2
  1093.2 17.6 %copy-start.25 = (pred[256]{0:T(512)(128)(4,1)S(1)}, pred[256]{0:T(512)(128)(4,1)}, u32[]{:S(2)}) copy-start(pred[256]{0:T(512)(128)(4,1)} %iota_compare_fusion.4) | copy-start | bytes 772
  1129.1 7.8 copy-start.1
  (11 other events, 18.5 us)
Sparse Core Ops, SparseCore 0:
  13.4 34.4 all-gather.2
  500.2 34.1 all-gather.4
where the time goes:
time: 1150 us; the launch traced here: 1140 us
  other arithmetic  950 us (83%)
  matrix products  88.8 us (8%)
  local copies, waits for them, and re-layouts  66.7 us (6%)
  starting transfers between devices  17.3 us (2%)
  between operations  15.8 us (1%)
    another operation x33, other arithmetic, body(): node_factor = jnp.linalg.cholesky(node_gram)  413 us
    another operation x21, other arithmetic, retransfer(): lax.linalg.triangular_solve(parent_factor, flipped(carried), left_side=Tr...  335 us
    another operation x2, other arithmetic, body(): factor = jnp.linalg.cholesky(leaf_gram)  94.7 us
    another operation x2, other arithmetic, body(): lax.linalg.triangular_solve(factor, flipped(leaf_basis), left_side=True,...  80 us
    dot_general x25, matrix products, transpose_times(): return jnp.einsum('...ba,...bc->...ac', left, right, precision=highest)  45.4 us
    unnamed x61, local copies, waits for them, and re-layouts  30.2 us
    dot_general x12, matrix products, times_right(): return jnp.einsum('...ab,...bc->...ac', left, right, precision=highest)  27.5 us
  transfers between devices with their start and end apart: 9, of which 3 were waited for; matrix products, arithmetic and copies ran while one was open for 58% of the time, Pallas kernels for 0%

commit v1 on v0

v1 whole, which is shorter than its diff:
```python
import jax
import jax.numpy as jnp
from jax import lax
from jax.experimental import pallas as pl
from jax.experimental.pallas import tpu as pltpu
from jax.sharding import PartitionSpec as P

HIGH = lax.Precision.HIGHEST
F32 = jnp.float32
N = 64


def nn(a, b):
    return lax.dot_general(a, b, (((1,), (0,)), ((), ())), precision=HIGH, preferred_element_type=F32)


def tn(a, b):
    return lax.dot_general(a, b, (((0,), (0,)), ((), ())), precision=HIGH, preferred_element_type=F32)


def nt(a, b):
    return lax.dot_general(a, b, (((1,), (1,)), ((), ())), precision=HIGH, preferred_element_type=F32)


def sandwich(e, g):
    return tn(e, nn(g, e))


def local_tree(pos_ref, basis_ref, lt_ref, it_ref, gram_ref, img_ref, tmp):
    blk = pos_ref[1]
    for c in range(16):
        b = basis_ref[c]
        g = tn(b, b)
        gram_ref[c] = g
        tmp[c] = sandwich(lt_ref[c], g)
    at, src = 16, 0
    for count in (8, 4, 2, 1):
        for n in range(count):
            g = tmp[src + 2 * n] + tmp[src + 2 * n + 1]
            gram_ref[at + n] = g
            m = sandwich(it_ref[4 * count - 1 + count * blk + n], g)
            if count == 1:
                img_ref[...] = m
                gram_ref[31] = g
            else:
                tmp[src + 2 * count + n] = m
        src += 2 * count
        at += count


def run_local_tree(pos, basis, lt, it):
    vm = pl.BlockSpec(memory_space=pltpu.VMEM)
    return pl.pallas_call(
        local_tree,
        out_shape=(jax.ShapeDtypeStruct((32, N, N), F32), jax.ShapeDtypeStruct((N, N), F32)),
        in_specs=[pl.BlockSpec(memory_space=pltpu.SMEM), vm, vm, vm],
        out_specs=(vm, vm),
        scratch_shapes=[pltpu.VMEM((32, N, N), F32)],
        compiler_params=pltpu.CompilerParams(vmem_limit_bytes=40 * 2**20),
    )(pos, basis, lt, it)


def eliminate(a_ref, w_ref, lanes):
    sub = lax.broadcasted_iota(jnp.int32, (8, lanes), 0)

    def bc(x, i):
        return jnp.broadcast_to(x[i:i + 1, :], (8, lanes))

    for p in range(8):
        k0 = 8 * p
        d = [a_ref[k0 + i, k0:k0 + 8, :] for i in range(8)]
        r = []
        coef = {}
        for k in range(8):
            piv = bc(d[k], k)
            y = lax.rsqrt(piv)
            y = y * (1.5 - 0.5 * piv * y * y)
            r.append(y)
            d[k] = d[k] * y
            for i in range(k + 1, 8):
                coef[k, i] = bc(d[k], i)
                d[i] = d[i] - coef[k, i] * d[k]
        for i in range(8):
            a_ref[k0 + i, k0:k0 + 8, :] = d[i]

        def solve(x):
            for k in range(8):
                x[k] = x[k] * r[k]
                for i in range(k + 1, 8):
                    x[i] = x[i] - coef[k, i] * x[k]
            return x

        for jb in range(p + 1, 8):
            x = solve([a_ref[k0 + i, 8 * jb:8 * jb + 8, :] for i in range(8)])
            for i in range(8):
                a_ref[k0 + i, 8 * jb:8 * jb + 8, :] = x[i]
        for jb in range(p + 1):
            if jb < p:
                x = [w_ref[k0 + i, 8 * jb:8 * jb + 8, :] for i in range(8)]
            else:
                x = [jnp.where(sub == i, F32(1), F32(0)) for i in range(8)]
            x = solve(x)
            for i in range(8):
                w_ref[k0 + i, 8 * jb:8 * jb + 8, :] = x[i]

        for ib in range(p + 1, 8):
            def step(t, _, ib=ib, p=p, k0=k0):
                i = 8 * ib + t
                cs = [jnp.broadcast_to(a_ref[k0 + k, pl.ds(i, 1), :], (8, lanes)) for k in range(8)]
                for jb in range(ib, 8):
                    acc = a_ref[i, 8 * jb:8 * jb + 8, :]
                    for k in range(8):
                        acc = acc - cs[k] * a_ref[k0 + k, 8 * jb:8 * jb + 8, :]
                    a_ref[i, 8 * jb:8 * jb + 8, :] = acc
                for jb in range(p + 1):
                    acc = w_ref[i, 8 * jb:8 * jb + 8, :] if jb < p else jnp.zeros((8, lanes), F32)
                    for k in range(8):
                        acc = acc - cs[k] * w_ref[k0 + k, 8 * jb:8 * jb + 8, :]
                    w_ref[i, 8 * jb:8 * jb + 8, :] = acc
                return 0
            lax.fori_loop(0, 8, step, 0)


def chain(m_ref, it_ref, up_ref, g_ref, quad, octet, four, send_sem, recv_sem):
    leaf, blk = lax.axis_index("leaf"), lax.axis_index("blk")
    low, high = leaf % 8, leaf // 8
    near = [({"leaf": leaf, "blk": (blk + i) % 4}) for i in range(1, 4)]
    mid = [({"leaf": high * 8 + (low + i) % 8, "blk": blk}) for i in range(1, 8)]
    far = [({"leaf": ((high + i) % 4) * 8 + low, "blk": blk}) for i in range(1, 4)]
    peers = near + mid + far
    barrier = pltpu.get_barrier_semaphore()
    for peer in peers:
        pl.semaphore_signal(barrier, inc=1, device_id=peer, device_id_type=pl.DeviceIdType.MESH)
    pl.semaphore_wait(barrier, len(peers))

    def exchange(value, slots, place, group, base):
        slots[place] = value
        copies = []
        for t, peer in enumerate(group):
            c = pltpu.make_async_remote_copy(
                src_ref=slots.at[place], dst_ref=slots.at[place],
                send_sem=send_sem.at[base + t], recv_sem=recv_sem.at[base + t],
                device_id=peer, device_id_type=pl.DeviceIdType.MESH)
            c.start()
            copies.append(c)
        for c in copies:
            c.wait()

    exchange(m_ref[...], quad, blk, near, 0)
    root = None
    for n in range(2):
        g = quad[2 * n] + quad[2 * n + 1]
        g_ref[n] = g
        m = sandwich(it_ref[1 + n], g)
        root = m if root is None else root + m
    g_ref[2] = root
    exchange(sandwich(it_ref[0], root), octet, low, mid, 3)
    first = [octet[2 * n] + octet[2 * n + 1] for n in range(4)]
    g_ref[3] = octet[low // 2 * 2] + octet[low // 2 * 2 + 1]
    images = [sandwich(up_ref[high * 8 + 2 * n], first[n]) for n in range(4)]
    second = [images[2 * n] + images[2 * n + 1] for n in range(2)]
    g_ref[4] = jnp.where(low < 4, second[0], second[1])
    images = [sandwich(up_ref[high * 8 + 4 * n + 1], second[n]) for n in range(2)]
    third = images[0] + images[1]
    g_ref[5] = third
    exchange(sandwich(up_ref[high * 8 + 3], third), four, high, far, 10)
    fourth = [four[2 * n] + four[2 * n + 1] for n in range(2)]
    g_ref[6] = jnp.where(high < 2, fourth[0], fourth[1])
    images = [sandwich(up_ref[16 * n + 7], fourth[n]) for n in range(2)]
    g_ref[7] = images[0] + images[1]


def run_chain(m, it, up):
    vm = pl.BlockSpec(memory_space=pltpu.VMEM)
    return pl.pallas_call(
        chain,
        out_shape=jax.ShapeDtypeStruct((8, N, N), F32),
        in_specs=[vm, vm, vm],
        out_specs=vm,
        scratch_shapes=[
            pltpu.VMEM((4, N, N), F32), pltpu.VMEM((8, N, N), F32), pltpu.VMEM((4, N, N), F32),
            pltpu.SemaphoreType.DMA((13,)), pltpu.SemaphoreType.DMA((13,)),
        ],
        compiler_params=pltpu.CompilerParams(collective_id=0, has_side_effects=True, vmem_limit_bytes=40 * 2**20),
    )(m, it, up)


def factors(pos_ref, g1_ref, g2_ref, basis_ref, lt_ref, it_ref, up_ref,
            orth_ref, newleaf_ref, pack_ref, shared_ref, upper_ref, upack_ref, a, w, u):
    leaf, blk = pos_ref[0], pos_ref[1]

    def load(k, _):
        x = jnp.concatenate([g1_ref[pl.ds(k, 32, stride=N), :], g2_ref[pl.ds(k, 8, stride=N), :]], axis=0)
        a[k] = x.T
        return 0
    lax.fori_loop(0, N, load, 0, unroll=4)
    eliminate(a, w, 40)
    col = lax.broadcasted_iota(jnp.int32, (N, 40), 0)

    def save(k, _):
        u[0, pl.ds(k, 40, stride=N), :] = jnp.where(col >= k, a[k], F32(0)).T
        u[1, pl.ds(k, 40, stride=N), :] = jnp.where(col <= k, w[k], F32(0)).T
        return 0
    lax.fori_loop(0, N, save, 0, unroll=4)

    def up(i):
        return u[0, pl.ds(i * N, N), :]

    def inverse(i):
        return u[1, pl.ds(i * N, N), :]

    for c in range(8):
        upack_ref[c] = jnp.concatenate([up(2 * c), up(2 * c + 1)], axis=1)
    for c in range(16):
        orth_ref[c] = nt(basis_ref[c], inverse(c))
        newleaf_ref[c] = nt(nn(up(c), lt_ref[c]), inverse(16 + c // 2))
    done = []
    at = 16
    for count in (8, 4, 2, 1):
        for n in range(count):
            e = it_ref[4 * count - 1 + count * blk + n]
            parent = at + count + n // 2 if count > 1 else 32 + blk // 2
            done.append(nt(nn(up(at + n), e), inverse(parent)))
        at += count
    done.append(done[-1])
    for c in range(8):
        pack_ref[c] = jnp.concatenate([done[2 * c], done[2 * c + 1]], axis=1)
    shared_ref[0] = nt(nn(up(34), it_ref[0]), inverse(35))
    for n in range(2):
        shared_ref[1 + n] = nt(nn(up(32 + n), it_ref[1 + n]), inverse(34))
    level = jnp.where(leaf % 2 == 1, 1, jnp.where(leaf % 4 == 2, 2, jnp.where(leaf % 8 == 4, 3, jnp.where(leaf % 16 == 8, 4, 5))))
    carried = nn(up(34 + level), up_ref[jnp.maximum(leaf - 1, 0)])
    renewed = nt(carried, inverse(jnp.minimum(35 + level, 39)))
    upper_ref[0] = jnp.where(leaf == 0, up(39), jnp.where(leaf == 16, carried, renewed))


def run_factors(pos, g1, g2, basis, lt, it, up):
    vm = pl.BlockSpec(memory_space=pltpu.VMEM)
    sd = jax.ShapeDtypeStruct
    return pl.pallas_call(
        factors,
        out_shape=(sd((16, N, N), F32), sd((16, N, N), F32), sd((8, N, 2 * N), F32), sd((3, N, N), F32),
                   sd((1, N, N), F32), sd((8, N, 2 * N), F32)),
        in_specs=[pl.BlockSpec(memory_space=pltpu.SMEM)] + [vm] * 6,
        out_specs=(vm,) * 6,
        scratch_shapes=[pltpu.VMEM((N, N, 40), F32), pltpu.VMEM((N, N, 40), F32), pltpu.VMEM((2, 40 * N, N), F32)],
        compiler_params=pltpu.CompilerParams(vmem_limit_bytes=48 * 2**20),
    )(pos, g1.reshape(32 * N, N), g2.reshape(8 * N, N), basis, lt, it, up)


def spread(u_ref, t_ref, all_u, all_t, send_sem, recv_sem, local_sem):
    leaf, blk = lax.axis_index("leaf"), lax.axis_index("blk")
    near = [{"leaf": leaf, "blk": (blk + i) % 4} for i in range(1, 4)]
    right = {"leaf": (leaf + 1) % 32, "blk": blk}
    left = {"leaf": (leaf + 31) % 32, "blk": blk}
    barrier = pltpu.get_barrier_semaphore()
    for peer in near + [right, left]:
        pl.semaphore_signal(barrier, inc=1, device_id=peer, device_id_type=pl.DeviceIdType.MESH)
    pl.semaphore_wait(barrier, 5)

    def push(src, dst, sem, peer):
        c = pltpu.make_async_remote_copy(
            src_ref=src, dst_ref=dst, send_sem=send_sem.at[sem], recv_sem=recv_sem.at[sem],
            device_id=peer, device_id_type=pl.DeviceIdType.MESH)
        c.start()
        return c

    own_u = pltpu.make_async_copy(u_ref, all_u.at[1, blk], local_sem.at[0])
    own_t = pltpu.make_async_copy(t_ref, all_t.at[blk], local_sem.at[1])
    own_u.start()
    own_t.start()
    hops = [push(u_ref, all_u.at[1, blk], i, near[i]) for i in (0, 2, 1)]
    rest = [push(u_ref, all_u.at[0, blk], 3, right), push(u_ref, all_u.at[2, blk], 4, left)]
    rest += [push(t_ref, all_t.at[blk], 5 + i, near[i]) for i in (0, 2, 1)]
    for c, i in zip(hops, (1, 3, 2)):
        c.wait_recv()
        got = (blk + 4 - i) % 4
        rest.append(push(all_u.at[1, got], all_u.at[0, got], 8 + 2 * (i - 1), right))
        rest.append(push(all_u.at[1, got], all_u.at[2, got], 9 + 2 * (i - 1), left))
    own_u.wait()
    own_t.wait()
    for c in hops:
        c.wait_send()
    for c in rest:
        c.wait()


def run_spread(u, t):
    vm = pl.BlockSpec(memory_space=pltpu.VMEM)
    sd = jax.ShapeDtypeStruct
    return pl.pallas_call(
        spread,
        out_shape=(sd((3, 4, 8, N, 2 * N), F32), sd((4, 8, N, 2 * N), F32)),
        in_specs=[vm, vm],
        out_specs=(vm, vm),
        scratch_shapes=[pltpu.SemaphoreType.DMA((14,)), pltpu.SemaphoreType.DMA((14,)), pltpu.SemaphoreType.DMA((2,))],
        compiler_params=pltpu.CompilerParams(collective_id=1, has_side_effects=True, vmem_limit_bytes=40 * 2**20),
    )(u, t)


BF = jnp.bfloat16


def split(x):
    h = x.astype(BF).astype(F32)
    return h, (x - h).astype(BF).astype(F32)


def project(pair_ref, count_ref, c_ref, u_ref, t_ref, shared_ref, out_ref, inner_ref, s, cols, rows):
    lane = lax.broadcasted_iota(jnp.int32, (N, 2 * N), 1)
    first = lane < N

    def turn(a, _):
        x = jnp.concatenate([c_ref[a, :, 0:128], c_ref[a, :, 128:256]], axis=0)
        s[pl.ds(a, 128, stride=N), :] = x.T
        return 0
    lax.fori_loop(0, N, turn, 0, unroll=2)

    def cut(x):
        h, l = split(x)
        return h, l, pltpu.roll(h, N, 1), pltpu.roll(l, N, 1)

    def prepare(p, _):
        h, l, hr, lr = cut(u_ref[p])
        cols[2 * p] = jnp.concatenate([jnp.where(first, h, hr), jnp.where(first, l, lr)], axis=1).astype(BF)
        cols[2 * p + 1] = jnp.concatenate([jnp.where(first, hr, h), jnp.where(first, lr, l)], axis=1).astype(BF)
        return 0
    lax.fori_loop(0, 96, prepare, 0, unroll=2)

    def prepare_rows(p, _):
        h, l, hr, lr = cut(u_ref[32 + p])
        rows[2 * p] = jnp.where(first, h, lr).astype(BF)
        rows[2 * p + 1] = jnp.where(first, hr, l).astype(BF)
        return 0
    lax.fori_loop(0, 32, prepare_rows, 0, unroll=2)

    base = pair_ref[2, 0]

    def slot(k, d):
        i = jnp.clip(pair_ref[0, k] - base, 0, 63)
        j = jnp.clip(pair_ref[1, k] - base + 64, 0, 191)
        d = d.astype(BF)
        y = lax.dot_general(jnp.concatenate([d, d], axis=1), cols[j], (((1,), (1,)), ((), ())), preferred_element_type=F32)
        h = y.astype(BF)
        l = (y - h.astype(F32)).astype(BF)
        r = rows[i]
        return lax.dot_general(jnp.concatenate([r, r], axis=1), jnp.concatenate([h, h, l, l], axis=0),
                               (((1,), (0,)), ((), ())), preferred_element_type=F32)

    def both(k, _):
        at = pl.ds(pl.multiple_of(k * N, N), N)
        h, l, hr, lr = cut(s[at, :])
        s[at, :] = jnp.concatenate([slot(k, jnp.where(first, h, lr)), slot(k + 128, jnp.where(first, hr, l))], axis=1)
        return 0
    lax.fori_loop(0, 128, both, 0, unroll=4)

    def back(a, _):
        x = s[pl.ds(a, 128, stride=N), :].T
        out_ref[a, :, 0:128] = jnp.where(lane < count_ref[0], x[:N], F32(0))
        out_ref[a, :, 128:256] = jnp.where(lane + 128 < count_ref[0], x[N:], F32(0))
        return 0
    lax.fori_loop(0, N, back, 0, unroll=2)

    for n in range(3):
        inner_ref[n] = shared_ref[n]
    for b in range(4):
        at = 0
        for count in (8, 4, 2, 1):
            for n in range(count):
                inner_ref[4 * count - 1 + count * b + n] = t_ref[b, at // 2, :, (at % 2) * N:(at % 2) * N + N]
                at += 1


def run_project(pairs, counts, base, coupling, u, t, shared):
    vm = pl.BlockSpec(memory_space=pltpu.VMEM)
    sm = pl.BlockSpec(memory_space=pltpu.SMEM)
    sd = jax.ShapeDtypeStruct
    table = jnp.concatenate([pairs.T, jnp.broadcast_to(base, (1, 256))], axis=0)
    out, inner = pl.pallas_call(
        project,
        out_shape=(sd((N, N, 256), F32), sd((63, N, N), F32)),
        in_specs=[sm, sm, vm, vm, vm, vm],
        out_specs=(vm, vm),
        scratch_shapes=[pltpu.VMEM((128 * N, 2 * N), F32), pltpu.VMEM((192, N, 4 * N), BF), pltpu.VMEM((64, N, 2 * N), BF)],
        compiler_params=pltpu.CompilerParams(vmem_limit_bytes=60 * 2**20),
    )(table, counts, jnp.transpose(coupling, (1, 2, 0)), u.reshape(96, N, 2 * N), t, shared)
    return jnp.transpose(out, (2, 0, 1)), inner


def body(leaf_basis, leaf_transfer, inner_transfer, upper_transfer, coupling, pairs, counts):
    leaf, blk = lax.axis_index("leaf"), lax.axis_index("blk")
    pos = jnp.stack([leaf, blk]).astype(jnp.int32)
    g1, m = run_local_tree(pos, leaf_basis, leaf_transfer, inner_transfer)
    g2 = run_chain(m, inner_transfer, upper_transfer)
    orth, new_leaf, pack, shared, upper, upack = run_factors(
        pos, g1, g2, leaf_basis, leaf_transfer, inner_transfer, upper_transfer)
    all_u, all_t = run_spread(upack, pack)
    out, inner = run_project(pairs, counts, (leaf * 64).astype(jnp.int32), coupling, all_u, all_t, shared)
    return orth, new_leaf, inner, upper, out


def solution(mesh):
    in_specs = (
        P(("leaf", "blk"), None, None),
        P(("leaf", "blk"), None, None),
        P("leaf", None, None),
        P(),
        P(("leaf", "blk"), None, None),
        P(("leaf", "blk"), None),
        P(("leaf", "blk")),
    )
    out_specs = (
        P(("leaf", "blk"), None, None),
        P(("leaf", "blk"), None, None),
        P("leaf", None, None),
        P("leaf", None, None),
        P(("leaf", "blk"), None, None),
    )
    return jax.shard_map(body, mesh=mesh, in_specs=in_specs, out_specs=out_specs, check_vma=False)
```

time: 1150 us -> 130 us (0.11)
  other arithmetic: 950 us -> 0.08 us
  Pallas kernels: 0 us -> 119 us
  matrix products: 88.8 us -> 0 us
  local copies, waits for them, and re-layouts: 66.7 us -> 7.57 us
  starting transfers between devices: 17.3 us -> 0 us
  between operations: 15.8 us -> 1.35 us
    another operation x58 -> x1, other arithmetic: 923 us -> 0.08 us  [body(): pos = jnp.stack([leaf, blk]).astype(jnp.int32)]
    pallas_call x0 -> x5, Pallas kernels: none -> 119 us  [the longest x1 38.5 us: run_project(): pl.pallas_call(project, out_shape=(sd((N, N, 256), F32), sd((63, N, N), F...]
    dot_general x37 -> x0, matrix products: 72.9 us -> none  [the longest x25 45.4 us: transpose_times(): return jnp.einsum('...ba,...bc->...ac', left, right, precision=highest)]
    unnamed x61 -> x20, local copies, waits for them, and re-layouts: 30.2 us -> 6.3 us
    ppermute x7 -> x0, starting transfers between devices: 17.2 us -> none  [the longest x5 9.81 us: swapped(): lax.ppermute(value, axis, [(i, i ^ 1 << bit) for i in range(lax.axis_size...]
    another operation x12 -> x0, matrix products: 15.9 us -> none  [the longest x11 12.8 us: retransfer(): lax.linalg.triangular_solve(parent_factor, flipped(carried), left_side=Tr...]
    gather x2 -> x0, local copies, waits for them, and re-layouts: 13.4 us -> none  [the longest x1 7.23 us: body(): col_factor = nearby[col_local]]
    div x12 -> x0, other arithmetic: 12.8 us -> none  [the longest x11 12.7 us: body(): node_factor = jnp.linalg.cholesky(node_gram)]
  transfers between devices with their start and end apart: 9 -> 0, of which waited for: 3 -> 0; matrix products, arithmetic and copies ran while one was open for 58% -> 0% of each run, Pallas kernels for 0% -> 0%
where the time goes in v1:
time: 130 us; the launch traced here: 128 us
  Pallas kernels  119 us (92%)
  local copies, waits for them, and re-layouts  7.57 us (6%)
  between operations  1.35 us (1%)
    pallas_call x1, Pallas kernels, run_project(): pl.pallas_call(project, out_shape=(sd((N, N, 256), F32), sd((63, N, N), F...  38.5 us
    pallas_call x1, Pallas kernels, run_spread(): pl.pallas_call(spread, out_shape=(sd((3, 4, 8, N, 2 * N), F32), sd((4, 8,...  26.9 us
    pallas_call x1, Pallas kernels, run_factors(): pl.pallas_call(factors, out_shape=(sd((16, N, N), F32), sd((16, N, N), F3...  25.9 us
    pallas_call x1, Pallas kernels, run_chain(): pl.pallas_call(chain, out_shape=jax.ShapeDtypeStruct((8, N, N), F32), in_...  22.4 us
    unnamed x20, local copies, waits for them, and re-layouts  6.3 us
    pallas_call x1, Pallas kernels, run_local_tree(): pl.pallas_call(local_tree, out_shape=(jax.ShapeDtypeStruct((32, N, N), F3...  5.84 us

profile of v1, /device:TPU:1, one launch (start us, length us, event | category | flops | bytes accessed | tf_op | source)
XLA Modules:
  0.0 128.5 jit_solution(11789765930276021941)
XLA Ops:
  1.3 0.1 pad_add_fusion.pos_ref
  1.4 1.3 concatenate.3.pair_ref
  2.6 0.0 copy-start
  2.6 1.6 %copy-done = f32[63,64,64]{2,1,0:T(8,128)S(1)} copy-done((f32[63,64,64]{2,1,0:T(8,128)S(1)}, f32[63,64,64]{2,1,0:T(8,128)}, u32[]{:S(2)}) %copy-start) | copy-done | bytes 1032216
  4.2 0.0 copy-start.4
  4.2 1.0 copy-done.4
  5.2 0.0 copy-start.6
  5.3 1.0 copy-done.6
  6.3 0.0 copy-start.1
  6.3 0.0 copy-start.2
  6.3 0.0 copy-start.5
  6.3 5.8 %shard_map.110 = (f32[32,64,64]{2,1,0:T(8,128)S(1)}, f32[64,64]{1,0:T(8,128)S(1)}) custom-call(s32[2]{0:T(128)S(1)} %pad_add_fusion.pos_ref, f32[16,64,64]{2,1,0:T(8,128)S(1)} %copy-done.4, f32[16,64,64]{2,1,0:T(8,128)S(1)} %copy-done.6, f32[63,64,64]{2,1,0:T(8,128)S(1)} %copy-done), custom_call_target="tpu_custom_call" | custom-call | tf_op jit(solution)/shard_map/pallas_call | solution.py:53
  12.1 0.0 copy-done.1
  12.1 0.0 copy-done.2
  12.2 22.4 %shard_map.111 = f32[8,64,64]{2,1,0:T(8,128)S(1)} custom-call(f32[64,64]{1,0:T(8,128)S(1)} %get-tuple-element.18.m_ref, f32[63,64,64]{2,1,0:T(8,128)S(1)} %copy-done.1, f32[31,64,64]{2,1,0:T(8,128)S(1)} %copy-done.2), custom_call_target="tpu_custom_call" | custom-call | tf_op jit(solution)/shard_map/pallas_call | solution.py:175
  34.5 0.0 copy-done.5
  34.5 0.0 copy-done.7
  34.5 25.9 %shard_map.112 = (f32[16,64,64]{2,1,0:T(8,128)}, f32[16,64,64]{2,1,0:T(8,128)}, f32[8,64,128]{2,1,0:T(8,128)S(1)}, f32[3,64,64]{2,1,0:T(8,128)S(1)}, f32[1,64,64]{2,1,0:T(8,128)}, /*index=5*/f32[8,64,128]{2,1,0:T(8,128)S(1)}) custom-call(s32[2]{0:T(128)S(1)} %pad_add_fusion.pos_ref, f32[2048,64]{1,0:T(8,128)S(1)} %bitcast.10, f32[512,64]{1,0:T(8,128)S(1)} %bitcast.9, ...), custom_call_target="tpu_custom_call" | custom-call | tf_op jit(solution)/shard_map/pallas_call | solution.py:240
  60.4 26.9 %shard_map.113 = (f32[3,4,8,64,128]{4,3,2,1,0:T(8,128)S(1)}, f32[4,8,64,128]{3,2,1,0:T(8,128)S(1)}) custom-call(f32[8,64,128]{2,1,0:T(8,128)S(1)} %get-tuple-element.21.u_ref, f32[8,64,128]{2,1,0:T(8,128)S(1)} %get-tuple-element.22.t_ref), custom_call_target="tpu_custom_call" | custom-call | tf_op jit(solution)/shard_map/pallas_call | solution.py:291
  87.3 0.0 copy-done.9
  87.3 0.0 copy-start.3
  87.3 1.6 %copy-done.3 = f32[3,4,8,64,128]{4,3,2,1,0:T(8,128)} copy-done((f32[3,4,8,64,128]{4,3,2,1,0:T(8,128)}, f32[3,4,8,64,128]{4,3,2,1,0:T(8,128)S(1)}, u32[]{:S(2)}) %copy-start.3) | copy-done | bytes 3145752
  88.9 1.0 copy-done.8
  89.9 38.5 %shard_map.114 = (f32[64,64,256]{2,1,0:T(8,128)}, f32[63,64,64]{2,1,0:T(8,128)}) custom-call(s32[3,256]{1,0:T(4,128)} %concatenate.3.pair_ref, s32[1]{0:T(128)S(6)} %copy.12.count_ref, f32[64,64,256]{2,1,0:T(8,128)} %bitcast.11, f32[96,64,128]{2,1,0:T(8,128)} %bitcast.8, f32[4,8,64,128]{3,2,1,0:T(8,128)} %copy-done.8, f32[3,64,64]{2,1,0:T(8,128)} %copy-done.9), custom_call_target="tpu_custom_call" | custom-call | tf_op jit(solution)/shard_map/pallas_call | solution.py:379
  (3 shorter events, 0.0 us)
Async XLA Ops:
  2.6 1.6 %copy-start = (f32[63,64,64]{2,1,0:T(8,128)S(1)}, f32[63,64,64]{2,1,0:T(8,128)}, u32[]{:S(2)}) copy-start(f32[63,64,64]{2,1,0:T(8,128)} %it_ref.5) | copy-start | bytes 3096580
  4.2 1.0 copy-start.4
  5.2 1.0 copy-start.6
  6.3 5.9 %copy-start.1 = (f32[63,64,64]{2,1,0:T(8,128)S(1)}, f32[63,64,64]{2,1,0:T(8,128)}, u32[]{:S(2)}) copy-start(f32[63,64,64]{2,1,0:T(8,128)} %it_ref.5) | copy-start | bytes 3096580
  6.3 5.9 %copy-start.2 = (f32[31,64,64]{2,1,0:T(8,128)S(1)}, f32[31,64,64]{2,1,0:T(8,128)}, u32[]{:S(2)}) copy-start(f32[31,64,64]{2,1,0:T(8,128)} %up_ref.3) | copy-start | bytes 1523716
  6.3 28.2 %copy-start.5 = (f32[16,64,64]{2,1,0:T(8,128)S(1)}, f32[16,64,64]{2,1,0:T(8,128)}, u32[]{:S(2)}) copy-start(f32[16,64,64]{2,1,0:T(8,128)} %basis_ref.3) | copy-start | bytes 786436
  6.3 28.2 %copy-start.7 = (f32[16,64,64]{2,1,0:T(8,128)S(1)}, f32[16,64,64]{2,1,0:T(8,128)}, u32[]{:S(2)}) copy-start(f32[16,64,64]{2,1,0:T(8,128)} %lt_ref.3) | copy-start | bytes 786436
  60.4 26.9 %copy-start.9 = (f32[3,64,64]{2,1,0:T(8,128)}, f32[3,64,64]{2,1,0:T(8,128)S(1)}, u32[]{:S(2)}) copy-start(f32[3,64,64]{2,1,0:T(8,128)S(1)} %get-tuple-element.25.shared_ref) | copy-start | bytes 147460
  87.3 1.6 %copy-start.3 = (f32[3,4,8,64,128]{4,3,2,1,0:T(8,128)}, f32[3,4,8,64,128]{4,3,2,1,0:T(8,128)S(1)}, u32[]{:S(2)}) copy-start(f32[3,4,8,64,128]{4,3,2,1,0:T(8,128)S(1)} %get-tuple-element.23) | copy-start | bytes 9437188
  88.9 1.0 copy-start.8

commit v2 on v0

v2 whole, which is shorter than its diff:
```python
import jax
import jax.numpy as jnp
from jax import lax
from jax.experimental import pallas as pl
from jax.experimental.pallas import tpu as pltpu
from jax.sharding import PartitionSpec as P

HIGH = lax.Precision.HIGHEST
F32 = jnp.float32
N = 64


def nn(a, b):
    return lax.dot_general(a, b, (((1,), (0,)), ((), ())), precision=HIGH, preferred_element_type=F32)


def tn(a, b):
    return lax.dot_general(a, b, (((0,), (0,)), ((), ())), precision=HIGH, preferred_element_type=F32)


def nt(a, b):
    return lax.dot_general(a, b, (((1,), (1,)), ((), ())), precision=HIGH, preferred_element_type=F32)


def sandwich(e, g):
    return tn(e, nn(g, e))


def local_tree(pos_ref, basis_ref, lt_ref, it_ref, gram_ref, img_ref, tmp):
    blk = pos_ref[1]
    for c in range(16):
        b = basis_ref[c]
        g = tn(b, b)
        gram_ref[c] = g
        tmp[c] = sandwich(lt_ref[c], g)
    at, src = 16, 0
    for count in (8, 4, 2, 1):
        for n in range(count):
            g = tmp[src + 2 * n] + tmp[src + 2 * n + 1]
            gram_ref[at + n] = g
            m = sandwich(it_ref[4 * count - 1 + count * blk + n], g)
            if count == 1:
                img_ref[...] = jnp.concatenate([g, m], axis=1)
                gram_ref[31] = g
            else:
                tmp[src + 2 * count + n] = m
        src += 2 * count
        at += count


def run_local_tree(pos, basis, lt, it):
    vm = pl.BlockSpec(memory_space=pltpu.VMEM)
    return pl.pallas_call(
        local_tree,
        out_shape=(jax.ShapeDtypeStruct((32, N, N), F32), jax.ShapeDtypeStruct((N, 2 * N), F32)),
        in_specs=[pl.BlockSpec(memory_space=pltpu.SMEM), vm, vm, vm],
        out_specs=(vm, vm),
        scratch_shapes=[pltpu.VMEM((32, N, N), F32)],
        compiler_params=pltpu.CompilerParams(vmem_limit_bytes=40 * 2**20),
    )(pos, basis, lt, it)


LANES = 128
COPIES = 29


def eliminate(a_ref, w_ref):
    sub = lax.broadcasted_iota(jnp.int32, (8, LANES), 0)

    def bc(x, i):
        return jnp.broadcast_to(x[i:i + 1, :], (8, LANES))

    def panel(p):
        k0 = 8 * p
        d = [a_ref[k0 + i, k0:k0 + 8, :] for i in range(8)]
        r, coef = [], {}
        for k in range(8):
            piv = bc(d[k], k)
            y = lax.rsqrt(piv)
            y = y * (1.5 - 0.5 * piv * y * y)
            r.append(y)
            d[k] = d[k] * y
            for i in range(k + 1, 8):
                coef[k, i] = bc(d[k], i)
                d[i] = d[i] - coef[k, i] * d[k]
        for i in range(8):
            a_ref[k0 + i, k0:k0 + 8, :] = d[i]

        def solve(x):
            for k in range(8):
                x[k] = x[k] * r[k]
                for i in range(k + 1, 8):
                    x[i] = x[i] - coef[k, i] * x[k]
            return x

        for jb in range(p + 1, 8):
            x = solve([a_ref[k0 + i, 8 * jb:8 * jb + 8, :] for i in range(8)])
            for i in range(8):
                a_ref[k0 + i, 8 * jb:8 * jb + 8, :] = x[i]
        for jb in range(p + 1):
            if jb < p:
                x = [w_ref[k0 + i, 8 * jb:8 * jb + 8, :] for i in range(8)]
            else:
                x = [jnp.where(sub == i, F32(1), F32(0)) for i in range(8)]
            x = solve(x)
            for i in range(8):
                w_ref[k0 + i, 8 * jb:8 * jb + 8, :] = x[i]

    def trail(p, row, targets):
        k0 = 8 * p
        for g in range(0, len(targets), 2):
            group = targets[g:g + 2]
            acc = {}
            for t, (ref, jb, fresh) in enumerate(group):
                for i in range(8):
                    acc[t, i] = jnp.zeros((8, LANES), F32) if fresh else ref[row + i, 8 * jb:8 * jb + 8, :]
            for k in range(8):
                pivots = [ref[k0 + k, 8 * jb:8 * jb + 8, :] for ref, jb, _ in group]
                for i in range(8):
                    c = jnp.broadcast_to(a_ref[k0 + k, pl.ds(row + i, 1), :], (8, LANES))
                    for t in range(len(group)):
                        acc[t, i] = acc[t, i] - c * pivots[t]
            for t, (ref, jb, _) in enumerate(group):
                for i in range(8):
                    ref[row + i, 8 * jb:8 * jb + 8, :] = acc[t, i]

    for p in range(8):
        panel(p)
        targets = [(a_ref, jb, False) for jb in range(p + 1, 8)] + [(w_ref, jb, jb == p) for jb in range(p + 1)]

        def step(ib, _):
            trail(p, 8 * ib, targets)
            return 0
        lax.fori_loop(p + 1, 8, step, 0)


def factor_stack(g_ref, u_ref, w_ref, a, w, n):
    def load(k, _):
        a[k, :, 0:n] = g_ref[pl.ds(k, n, stride=N), :].T
        return 0
    lax.fori_loop(0, N, load, 0, unroll=8)
    eliminate(a, w)
    col = lax.broadcasted_iota(jnp.int32, (N, n), 0)

    def save(k, _):
        u_ref[pl.ds(k, n, stride=N), :] = jnp.where(col >= k, a[k, :, 0:n], F32(0)).T
        w_ref[pl.ds(k, n, stride=N), :] = jnp.where(col <= k, w[k, :, 0:n], F32(0)).T
        return 0
    lax.fori_loop(0, N, save, 0, unroll=8)


def lower_factors(g_ref, u_ref, w_ref, pack_ref, a, w):
    factor_stack(g_ref, u_ref, w_ref, a, w, 32)
    for c in range(8):
        pack_ref[c] = jnp.concatenate([u_ref[2 * c * N:2 * c * N + N, :], u_ref[2 * c * N + N:2 * c * N + 2 * N, :]], axis=1)


def run_lower_factors(g):
    vm = pl.BlockSpec(memory_space=pltpu.VMEM)
    s = jax.ShapeDtypeStruct((32 * N, N), F32)
    return pl.pallas_call(
        lower_factors,
        out_shape=(s, s, jax.ShapeDtypeStruct((8, N, 2 * N), F32)),
        in_specs=[vm],
        out_specs=(vm, vm, vm),
        scratch_shapes=[pltpu.VMEM((N, N, LANES), F32)] * 2,
        compiler_params=pltpu.CompilerParams(vmem_limit_bytes=40 * 2**20),
    )(g.reshape(32 * N, N))


BF = jnp.bfloat16


def split(x):
    h = x.astype(BF).astype(F32)
    return h, (x - h).astype(BF).astype(F32)


def cut(x):
    h, l = split(x)
    return h, l, pltpu.roll(h, N, 1), pltpu.roll(l, N, 1)


def middle(table_ref, count_ref, gm_ref, pack_ref, u_ref, w_ref, basis_ref, lt_ref, it_ref, up_ref, c_ref,
           orth_ref, newleaf_ref, g_ref, inner_ref, out_ref,
           buf, s, r, cols, rows, all_u, all_t, quad, octet, four, send_sem, recv_sem, local_sem):
    leaf, blk = lax.axis_index("leaf"), lax.axis_index("blk")
    low, high = leaf % 8, leaf // 8
    zup, zdown, zfar = [{"leaf": leaf, "blk": (blk + i) % 4} for i in (1, 3, 2)]
    right = {"leaf": (leaf + 1) % 32, "blk": blk}
    left = {"leaf": (leaf + 31) % 32, "blk": blk}
    mid = [{"leaf": high * 8 + (low + i) % 8, "blk": blk} for i in range(1, 8)]
    far = [{"leaf": (high + i) % 4 * 8 + low, "blk": blk} for i in range(1, 4)]
    peers = [zup, zdown, zfar, right, left] + mid + far
    barrier = pltpu.get_barrier_semaphore()
    for peer in peers:
        pl.semaphore_signal(barrier, inc=1, device_id=peer, device_id_type=pl.DeviceIdType.MESH)
    fetch = pltpu.make_async_copy(c_ref, buf, local_sem.at[0])
    fetch.start()
    own_u = pltpu.make_async_copy(pack_ref, all_u.at[pl.ds((4 + blk) * 8, 8)], local_sem.at[1])
    own_u.start()
    used = []

    def push(src, dst, peer):
        i = len(used)
        c = pltpu.make_async_remote_copy(
            src_ref=src, dst_ref=dst, send_sem=send_sem.at[i], recv_sem=recv_sem.at[i],
            device_id=peer, device_id_type=pl.DeviceIdType.MESH)
        c.start()
        used.append(c)
        return c

    def block(d, b, start, count):
        return all_u.at[pl.ds((d * 4 + b) * 8 + start, count)]

    def u(i):
        return u_ref[i * N:i * N + N, :]

    def w(i):
        return w_ref[i * N:i * N + N, :]

    def orth(c):
        orth_ref[c] = nt(basis_ref[c], w(c))

    for c in range(8):
        orth(c)
    quad[blk] = gm_ref[...]
    pl.semaphore_wait(barrier, len(peers))

    quads = [push(quad.at[blk], quad.at[blk], peer) for peer in (zup, zdown, zfar)]
    u_up = push(pack_ref, block(1, blk, 0, 8), zup)
    u_down = push(pack_ref, block(1, blk, 0, 8), zdown)
    sides = [push(pack_ref, block(0, blk, 0, 8), right), push(pack_ref, block(2, blk, 0, 8), left)]
    for c in range(8, 16):
        orth(c)
    for c in range(16):
        newleaf_ref[c] = nt(nn(u(c), lt_ref[c]), w(16 + c // 2))

    for c in quads:
        c.wait_recv()
    root = None
    for n in range(2):
        g_ref[2 * n] = quad[2 * n, :, 0:N]
        g_ref[2 * n + 1] = quad[2 * n + 1, :, 0:N]
        g = quad[2 * n, :, N:2 * N] + quad[2 * n + 1, :, N:2 * N]
        g_ref[4 + n] = g
        m = sandwich(it_ref[1 + n], g)
        root = m if root is None else root + m
    g_ref[6] = root
    octet[low] = sandwich(it_ref[0], root)
    octets = [push(octet.at[low], octet.at[low], peer) for peer in mid]

    below, above, beyond = (blk + 3) % 4, (blk + 1) % 4, (blk + 2) % 4
    u_up.wait_recv()
    half_up = push(block(1, below, 0, 4), block(1, below, 0, 4), zup)
    u_down.wait_recv()
    half_down = push(block(1, above, 4, 4), block(1, above, 4, 4), zdown)
    for b in (below, above):
        sides += [push(block(1, b, 0, 8), block(0, b, 0, 8), right), push(block(1, b, 0, 8), block(2, b, 0, 8), left)]

    done, at = [], 16
    for count in (8, 4, 2):
        for n in range(count):
            e = it_ref[4 * count - 1 + count * blk + n]
            done.append(nt(nn(u(at + n), e), w(at + count + n // 2)))
        at += count
    for c in range(7):
        all_t[blk, c] = jnp.concatenate([done[2 * c], done[2 * c + 1]], axis=1)
    t_up = push(all_t.at[blk], all_t.at[blk], zup)
    t_down = push(all_t.at[blk], all_t.at[blk], zdown)

    for c in octets:
        c.wait_recv()
    first = [octet[2 * n] + octet[2 * n + 1] for n in range(4)]
    g_ref[7] = octet[low // 2 * 2] + octet[low // 2 * 2 + 1]
    images = [sandwich(up_ref[high * 8 + 2 * n], first[n]) for n in range(4)]
    second = [images[2 * n] + images[2 * n + 1] for n in range(2)]
    g_ref[8] = jnp.where(low < 4, second[0], second[1])
    images = [sandwich(up_ref[high * 8 + 4 * n + 1], second[n]) for n in range(2)]
    third = images[0] + images[1]
    g_ref[9] = third
    four[high] = sandwich(up_ref[high * 8 + 3], third)
    fours = [push(four.at[high], four.at[high], peer) for peer in far]

    half_up.wait_recv()
    half_down.wait_recv()
    sides += [push(block(1, beyond, 0, 8), block(0, beyond, 0, 8), right),
              push(block(1, beyond, 0, 8), block(2, beyond, 0, 8), left)]

    lane = lax.broadcasted_iota(jnp.int32, (N, 2 * N), 1)
    lower = lane < N
    fetch.wait()

    def turn(a, _):
        x = jnp.concatenate([buf[a, :, 0:128], buf[a, :, 128:256]], axis=0)
        s[pl.ds(a, 128, stride=N), :] = x.T
        return 0
    lax.fori_loop(0, N, turn, 0, unroll=8)

    for c in fours:
        c.wait_recv()
    fourth = [four[2 * n] + four[2 * n + 1] for n in range(2)]
    g_ref[10] = jnp.where(high < 2, fourth[0], fourth[1])
    images = [sandwich(up_ref[16 * n + 7], fourth[n]) for n in range(2)]
    for n in range(11, 16):
        g_ref[n] = images[0] + images[1]

    t_up.wait_recv()
    t_half_up = push(all_t.at[below, pl.ds(0, 4)], all_t.at[below, pl.ds(0, 4)], zup)
    t_down.wait_recv()
    t_half_down = push(all_t.at[above, pl.ds(4, 3)], all_t.at[above, pl.ds(4, 3)], zdown)

    def prepare(p, _):
        h, l, hr, lr = cut(all_u[p])
        cols[2 * p] = jnp.concatenate([jnp.where(lower, h, hr), jnp.where(lower, l, lr)], axis=1).astype(BF)
        cols[2 * p + 1] = jnp.concatenate([jnp.where(lower, hr, h), jnp.where(lower, lr, l)], axis=1).astype(BF)
        return 0

    def prepare_rows(p, _):
        h, l, hr, lr = cut(all_u[32 + p])
        rows[2 * p] = jnp.where(lower, h, lr).astype(BF)
        rows[2 * p + 1] = jnp.where(lower, hr, l).astype(BF)
        return 0
    own_u.wait()
    lax.fori_loop(0, 32, prepare_rows, 0, unroll=8)
    lax.fori_loop(32, 64, prepare, 0, unroll=8)
    for c in sides:
        c.wait_recv()
    lax.fori_loop(0, 32, prepare, 0, unroll=8)
    lax.fori_loop(64, 96, prepare, 0, unroll=8)

    base = leaf * 64

    def slot(k, d):
        i = jnp.clip(table_ref[0, k] - base, 0, 63)
        j = jnp.clip(table_ref[1, k] - base + 64, 0, 191)
        d = d.astype(BF)
        y = lax.dot_general(jnp.concatenate([d, d], axis=1), cols[j], (((1,), (1,)), ((), ())), preferred_element_type=F32)
        h = y.astype(BF)
        l = (y - h.astype(F32)).astype(BF)
        x = rows[i]
        return lax.dot_general(jnp.concatenate([x, x], axis=1), jnp.concatenate([h, h, l, l], axis=0),
                               (((1,), (0,)), ((), ())), preferred_element_type=F32)

    def both(k, _):
        at = pl.ds(pl.multiple_of(k * N, N), N)
        h, l, hr, lr = cut(s[at, :])
        r[at, :] = jnp.concatenate([slot(k, jnp.where(lower, h, lr)), slot(k + 128, jnp.where(lower, hr, l))], axis=1)
        return 0
    lax.fori_loop(0, 128, both, 0, unroll=16)

    live = count_ref[0]

    def back(a, _):
        x = r[pl.ds(a, 128, stride=N), :].T
        buf[a, :, 0:128] = jnp.where(lane < live, x[:N], F32(0))
        buf[a, :, 128:256] = jnp.where(lane + 128 < live, x[N:], F32(0))
        return 0
    stores = []
    for q in range(4):
        lax.fori_loop(16 * q, 16 * q + 16, back, 0, unroll=8)
        part = pl.ds(16 * q, 16)
        c = pltpu.make_async_copy(buf.at[part], out_ref.at[part], local_sem.at[2 + q])
        c.start()
        stores.append(c)

    t_half_up.wait_recv()
    t_half_down.wait_recv()
    for b in range(4):
        at = 0
        for count in (8, 4, 2):
            for n in range(count):
                inner_ref[4 * count - 8 + count * b + n] = all_t[b, at // 2, :, at % 2 * N:at % 2 * N + N]
                at += 1
    for c in used:
        c.wait_send()
    for c in stores:
        c.wait()


def run_middle(pairs, counts, gm, pack, u, w, basis, lt, it, up, coupling):
    vm = pl.BlockSpec(memory_space=pltpu.VMEM)
    sm = pl.BlockSpec(memory_space=pltpu.SMEM)
    hbm = pl.BlockSpec(memory_space=pl.ANY)
    sd = jax.ShapeDtypeStruct
    return pl.pallas_call(
        middle,
        out_shape=(sd((16, N, N), F32), sd((16, N, N), F32), sd((16, N, N), F32), sd((56, N, N), F32), sd((N, N, 256), F32)),
        in_specs=[sm, sm] + [vm] * 8 + [hbm],
        out_specs=(vm, vm, vm, vm, hbm),
        scratch_shapes=[
            pltpu.VMEM((N, N, 256), F32), pltpu.VMEM((128 * N, 2 * N), F32), pltpu.VMEM((128 * N, 2 * N), F32),
            pltpu.VMEM((192, N, 4 * N), BF), pltpu.VMEM((64, N, 2 * N), BF),
            pltpu.VMEM((96, N, 2 * N), F32), pltpu.VMEM((4, 7, N, 2 * N), F32),
            pltpu.VMEM((4, N, 2 * N), F32), pltpu.VMEM((8, N, N), F32), pltpu.VMEM((4, N, N), F32),
            pltpu.SemaphoreType.DMA((COPIES,)), pltpu.SemaphoreType.DMA((COPIES,)), pltpu.SemaphoreType.DMA((6,)),
        ],
        compiler_params=pltpu.CompilerParams(collective_id=0, has_side_effects=True, vmem_limit_bytes=58 * 2**20),
    )(pairs.T, counts, gm, pack, u, w, basis, lt, it, up, jnp.transpose(coupling, (1, 2, 0)))


def upper_factors(g_ref, it_ref, up_ref, pos_ref, orth_ref, leaf_ref, inner_ref, proj_ref,
                  orth_out, leaf_out, inner_out, proj_out, upper_ref, a, w, u_all, w_all, head, sem):
    leaf = pos_ref[0]
    copies = [pltpu.make_async_copy(orth_ref, orth_out, sem.at[0]), pltpu.make_async_copy(leaf_ref, leaf_out, sem.at[1]),
              pltpu.make_async_copy(inner_ref, inner_out.at[pl.ds(7, 56)], sem.at[2])]
    for q in range(4):
        part = pl.ds(16 * q, 16)
        copies.append(pltpu.make_async_copy(proj_ref.at[part], proj_out.at[part], sem.at[3 + q]))
    for c in copies:
        c.start()
    factor_stack(g_ref, u_all, w_all, a, w, 16)

    def u(i):
        return u_all[pl.ds(i * N, N), :]

    def inverse(i):
        return w_all[pl.ds(i * N, N), :]

    head[0] = nt(nn(u(6), it_ref[0]), inverse(7))
    for n in range(2):
        head[1 + n] = nt(nn(u(4 + n), it_ref[1 + n]), inverse(6))
    for n in range(4):
        head[3 + n] = nt(nn(u(n), it_ref[3 + n]), inverse(4 + n // 2))
    last = pltpu.make_async_copy(head, inner_out.at[pl.ds(0, 7)], sem.at[7])
    last.start()
    level = jnp.where(leaf % 2 == 1, 1, jnp.where(leaf % 4 == 2, 2, jnp.where(leaf % 8 == 4, 3, jnp.where(leaf % 16 == 8, 4, 5))))
    carried = nn(u(6 + level), up_ref[jnp.maximum(leaf - 1, 0)])
    renewed = nt(carried, inverse(jnp.minimum(7 + level, 11)))
    upper_ref[0] = jnp.where(leaf == 0, u(11), jnp.where(leaf == 16, carried, renewed))
    for c in copies:
        c.wait()
    last.wait()


def run_upper_factors(g, it, up, pos, orth, new_leaf, inner, proj):
    vm = pl.BlockSpec(memory_space=pltpu.VMEM)
    hbm = pl.BlockSpec(memory_space=pl.ANY)
    sd = jax.ShapeDtypeStruct
    return pl.pallas_call(
        upper_factors,
        out_shape=(sd((16, N, N), F32), sd((16, N, N), F32), sd((63, N, N), F32), sd((N, N, 256), F32), sd((1, N, N), F32)),
        in_specs=[vm, vm, vm, pl.BlockSpec(memory_space=pltpu.SMEM)] + [hbm] * 4,
        out_specs=(hbm, hbm, hbm, hbm, vm),
        scratch_shapes=[pltpu.VMEM((N, N, LANES), F32)] * 2 + [pltpu.VMEM((16 * N, N), F32)] * 2 + [
            pltpu.VMEM((7, N, N), F32), pltpu.SemaphoreType.DMA((8,))],
        compiler_params=pltpu.CompilerParams(vmem_limit_bytes=40 * 2**20),
    )(g.reshape(16 * N, N), it, up, pos, orth, new_leaf, inner, proj)


def body(leaf_basis, leaf_transfer, inner_transfer, upper_transfer, coupling, pairs, counts):
    pos = jnp.stack([lax.axis_index("leaf"), lax.axis_index("blk")]).astype(jnp.int32)
    g1, gm = run_local_tree(pos, leaf_basis, leaf_transfer, inner_transfer)
    u, w, pack = run_lower_factors(g1)
    orth, new_leaf, g2, inner, proj = run_middle(
        pairs, counts, gm, pack, u, w, leaf_basis, leaf_transfer, inner_transfer, upper_transfer, coupling)
    orth, new_leaf, inner, proj, upper = run_upper_factors(
        g2, inner_transfer, upper_transfer, pos, orth, new_leaf, inner, proj)
    return orth, new_leaf, inner, upper, jnp.transpose(proj, (2, 0, 1))


def solution(mesh):
    in_specs = (
        P(("leaf", "blk"), None, None),
        P(("leaf", "blk"), None, None),
        P("leaf", None, None),
        P(),
        P(("leaf", "blk"), None, None),
        P(("leaf", "blk"), None),
        P(("leaf", "blk")),
    )
    out_specs = (
        P(("leaf", "blk"), None, None),
        P(("leaf", "blk"), None, None),
        P("leaf", None, None),
        P("leaf", None, None),
        P(("leaf", "blk"), None, None),
    )
    return jax.shard_map(body, mesh=mesh, in_specs=in_specs, out_specs=out_specs, check_vma=False)
```

time: 1150 us -> 92.8 us (0.08)
  other arithmetic: 950 us -> 0.08 us
  matrix products: 88.8 us -> 0 us
  Pallas kernels: 0 us -> 77.1 us
  local copies, waits for them, and re-layouts: 66.7 us -> 13.7 us
  starting transfers between devices: 17.3 us -> 0 us
  between operations: 15.8 us -> 1.54 us
    another operation x58 -> x1, other arithmetic: 923 us -> 0.08 us  [body(): jnp.stack([lax.axis_index('leaf'), lax.axis_index('blk')]).astype(jnp.int32)]
    pallas_call x0 -> x4, Pallas kernels: none -> 77.1 us  [the longest x1 50 us: run_middle(): pl.pallas_call(middle, out_shape=(sd((16, N, N), F32), sd((16, N, N), F32...]
    dot_general x37 -> x0, matrix products: 72.9 us -> none  [the longest x25 45.4 us: transpose_times(): return jnp.einsum('...ba,...bc->...ac', left, right, precision=highest)]
    ppermute x7 -> x0, starting transfers between devices: 17.2 us -> none  [the longest x5 9.81 us: swapped(): lax.ppermute(value, axis, [(i, i ^ 1 << bit) for i in range(lax.axis_size...]
    unnamed x61 -> x28, local copies, waits for them, and re-layouts: 30.2 us -> 13.7 us
    another operation x12 -> x0, matrix products: 15.9 us -> none  [the longest x11 12.8 us: retransfer(): lax.linalg.triangular_solve(parent_factor, flipped(carried), left_side=Tr...]
    gather x2 -> x0, local copies, waits for them, and re-layouts: 13.4 us -> none  [the longest x1 7.23 us: body(): col_factor = nearby[col_local]]
    div x12 -> x0, other arithmetic: 12.8 us -> none  [the longest x11 12.7 us: body(): node_factor = jnp.linalg.cholesky(node_gram)]
  transfers between devices with their start and end apart: 9 -> 0, of which waited for: 3 -> 0; matrix products, arithmetic and copies ran while one was open for 58% -> 0% of each run, Pallas kernels for 0% -> 0%
where the time goes in v2:
time: 92.8 us; the launch traced here: 92.4 us
  Pallas kernels  77.1 us (83%)
  local copies, waits for them, and re-layouts  13.7 us (15%)
  between operations  1.54 us (2%)
    pallas_call x1, Pallas kernels, run_middle(): pl.pallas_call(middle, out_shape=(sd((16, N, N), F32), sd((16, N, N), F32...  50 us
    unnamed x28, local copies, waits for them, and re-layouts  13.7 us
    pallas_call x1, Pallas kernels, run_upper_factors(): pl.pallas_call(upper_factors, out_shape=(sd((16, N, N), F32), sd((16, N,...  11.7 us
    pallas_call x1, Pallas kernels, run_lower_factors(): pl.pallas_call(lower_factors, out_shape=(s, s, jax.ShapeDtypeStruct((8, N...  9.46 us
    pallas_call x1, Pallas kernels, run_local_tree(): pl.pallas_call(local_tree, out_shape=(jax.ShapeDtypeStruct((32, N, N), F3...  5.92 us

profile of v2, /device:TPU:1, one launch (start us, length us, event | category | flops | bytes accessed | tf_op | source)
XLA Modules:
  0.0 92.4 jit_solution(2849731413009429701)
XLA Ops:
  1.3 0.1 pad_add_fusion.pos_ref
  1.4 0.0 copy-start
  1.4 1.6 %copy-done = f32[63,64,64]{2,1,0:T(8,128)S(1)} copy-done((f32[63,64,64]{2,1,0:T(8,128)S(1)}, f32[63,64,64]{2,1,0:T(8,128)}, u32[]{:S(2)}) %copy-start) | copy-done | bytes 1032216
  2.9 0.0 copy-start.4
  2.9 1.0 %copy-done.4 = f32[16,64,64]{2,1,0:T(8,128)S(1)} copy-done((f32[16,64,64]{2,1,0:T(8,128)S(1)}, f32[16,64,64]{2,1,0:T(8,128)}, u32[]{:S(2)}) %copy-start.4) | copy-done | bytes 262168
  4.0 1.0 %copy-done.5 = f32[16,64,64]{2,1,0:T(8,128)S(1)} copy-done((f32[16,64,64]{2,1,0:T(8,128)S(1)}, f32[16,64,64]{2,1,0:T(8,128)}, u32[]{:S(2)}) %copy-start.5) | copy-done | bytes 262168
  5.0 5.9 %shard_map.110 = (f32[32,64,64]{2,1,0:T(8,128)S(1)}, f32[64,128]{1,0:T(8,128)S(1)}) custom-call(s32[2]{0:T(128)S(1)} %pad_add_fusion.pos_ref, f32[16,64,64]{2,1,0:T(8,128)S(1)} %copy-done.4, f32[16,64,64]{2,1,0:T(8,128)S(1)} %copy-done.5, f32[63,64,64]{2,1,0:T(8,128)S(1)} %copy-done), custom_call_target="tpu_custom_call" | custom-call | tf_op jit(solution)/shard_map/pallas_call | solution.py:53
  10.9 0.0 copy-start.13
  11.0 0.6 copy-done.13
  11.6 9.5 %shard_map.111 = (f32[2048,64]{1,0:T(8,128)S(1)}, f32[2048,64]{1,0:T(8,128)S(1)}, f32[8,64,128]{2,1,0:T(8,128)S(1)}) custom-call(f32[2048,64]{1,0:T(8,128)S(1)} %bitcast.7), custom_call_target="tpu_custom_call" | custom-call | tf_op jit(solution)/shard_map/pallas_call | solution.py:161
  21.0 0.0 copy-start.7
  21.0 1.0 %copy-done.7 = f32[2048,64]{1,0:T(8,128)} copy-done((f32[2048,64]{1,0:T(8,128)}, f32[2048,64]{1,0:T(8,128)S(1)}, u32[]{:S(2)}) %copy-start.7) | copy-done | bytes 524312
  22.0 1.0 %copy-done.8 = f32[2048,64]{1,0:T(8,128)} copy-done((f32[2048,64]{1,0:T(8,128)}, f32[2048,64]{1,0:T(8,128)S(1)}, u32[]{:S(2)}) %copy-start.8) | copy-done | bytes 524312
  23.0 0.7 copy-done.12
  23.7 50.0 %shard_map.112 = (f32[16,64,64]{2,1,0:T(8,128)}, f32[16,64,64]{2,1,0:T(8,128)}, f32[16,64,64]{2,1,0:T(8,128)}, f32[56,64,64]{2,1,0:T(8,128)}, f32[64,64,256]{2,1,0:T(8,128)}) custom-call(s32[2,256]{1,0:T(2,128)} %bitcast.10, s32[1]{0:T(128)S(6)} %copy.12.count_ref, f32[64,128]{1,0:T(8,128)} %copy-done.13, f32[8,64,128]{2,1,0:T(8,128)} %copy-done.12, ...), custom_call_target="tpu_custom_call" | custom-call | tf_op jit(solution)/shard_map/pallas_call | solution.py:386
  73.7 0.0 copy-done.1
  73.7 0.0 copy-done.3
  73.7 0.0 copy-start.2
  73.7 2.2 %copy-done.2 = f32[64,64,256]{2,1,0:T(8,128)S(1)} copy-done((f32[64,64,256]{2,1,0:T(8,128)S(1)}, f32[64,64,256]{2,1,0:T(8,128)}, u32[]{:S(2)}) %copy-start.2) | copy-done | bytes 4194328
  75.9 1.5 %copy-done.6 = f32[56,64,64]{2,1,0:T(8,128)S(1)} copy-done((f32[56,64,64]{2,1,0:T(8,128)S(1)}, f32[56,64,64]{2,1,0:T(8,128)}, u32[]{:S(2)}) %copy-start.6) | copy-done | bytes 917528
  77.4 1.0 %copy-done.9 = f32[16,64,64]{2,1,0:T(8,128)S(1)} copy-done((f32[16,64,64]{2,1,0:T(8,128)S(1)}, f32[16,64,64]{2,1,0:T(8,128)}, u32[]{:S(2)}) %copy-start.9) | copy-done | bytes 262168
  78.5 1.0 %copy-done.10 = f32[16,64,64]{2,1,0:T(8,128)S(1)} copy-done((f32[16,64,64]{2,1,0:T(8,128)S(1)}, f32[16,64,64]{2,1,0:T(8,128)}, u32[]{:S(2)}) %copy-start.10) | copy-done | bytes 262168
  79.5 1.0 %copy-done.11 = f32[16,64,64]{2,1,0:T(8,128)S(1)} copy-done((f32[16,64,64]{2,1,0:T(8,128)S(1)}, f32[16,64,64]{2,1,0:T(8,128)}, u32[]{:S(2)}) %copy-start.11) | copy-done | bytes 262168
  80.6 11.7 %shard_map.113 = (f32[16,64,64]{2,1,0:T(8,128)}, f32[16,64,64]{2,1,0:T(8,128)}, f32[63,64,64]{2,1,0:T(8,128)}, f32[64,64,256]{2,1,0:T(8,128)}, f32[1,64,64]{2,1,0:T(8,128)}) custom-call(f32[1024,64]{1,0:T(8,128)S(1)} %bitcast.8, f32[63,64,64]{2,1,0:T(8,128)S(1)} %copy-done.1, f32[31,64,64]{2,1,0:T(8,128)S(1)} %copy-done.3, s32[2]{0:T(128)S(1)} %pad_add_fusion.pos_ref, ...), custom_call_target="tpu_custom_call" | custom-call | tf_op jit(solution)/shard_map/pallas_call | solution.py:440
  (9 shorter events, 0.0 us)
Async XLA Ops:
  1.4 1.6 %copy-start = (f32[63,64,64]{2,1,0:T(8,128)S(1)}, f32[63,64,64]{2,1,0:T(8,128)}, u32[]{:S(2)}) copy-start(f32[63,64,64]{2,1,0:T(8,128)} %it_ref.5) | copy-start | bytes 3096580
  2.9 1.0 %copy-start.4 = (f32[16,64,64]{2,1,0:T(8,128)S(1)}, f32[16,64,64]{2,1,0:T(8,128)}, u32[]{:S(2)}) copy-start(f32[16,64,64]{2,1,0:T(8,128)} %basis_ref.3) | copy-start | bytes 786436
  4.0 1.0 %copy-start.5 = (f32[16,64,64]{2,1,0:T(8,128)S(1)}, f32[16,64,64]{2,1,0:T(8,128)}, u32[]{:S(2)}) copy-start(f32[16,64,64]{2,1,0:T(8,128)} %lt_ref.3) | copy-start | bytes 786436
  10.9 0.6 copy-start.13
  21.0 1.0 %copy-start.7 = (f32[2048,64]{1,0:T(8,128)}, f32[2048,64]{1,0:T(8,128)S(1)}, u32[]{:S(2)}) copy-start(f32[2048,64]{1,0:T(8,128)S(1)} %get-tuple-element.23.u_ref) | copy-start | bytes 1572868
  22.0 1.0 %copy-start.8 = (f32[2048,64]{1,0:T(8,128)}, f32[2048,64]{1,0:T(8,128)S(1)}, u32[]{:S(2)}) copy-start(f32[2048,64]{1,0:T(8,128)S(1)} %get-tuple-element.24.w_ref) | copy-start | bytes 1572868
  23.0 0.7 copy-start.12
  23.7 50.0 %copy-start.1 = (f32[63,64,64]{2,1,0:T(8,128)S(1)}, f32[63,64,64]{2,1,0:T(8,128)}, u32[]{:S(2)}) copy-start(f32[63,64,64]{2,1,0:T(8,128)} %it_ref.5) | copy-start | bytes 3096580
  23.7 50.1 %copy-start.3 = (f32[31,64,64]{2,1,0:T(8,128)S(1)}, f32[31,64,64]{2,1,0:T(8,128)}, u32[]{:S(2)}) copy-start(f32[31,64,64]{2,1,0:T(8,128)} %up_ref.3) | copy-start | bytes 1523716
  73.7 2.2 %copy-start.2 = (f32[64,64,256]{2,1,0:T(8,128)S(1)}, f32[64,64,256]{2,1,0:T(8,128)}, u32[]{:S(2)}) copy-start(f32[64,64,256]{2,1,0:T(8,128)} %get-tuple-element.29.proj_ref) | copy-start | bytes 12582916
  75.9 1.5 %copy-start.6 = (f32[56,64,64]{2,1,0:T(8,128)S(1)}, f32[56,64,64]{2,1,0:T(8,128)}, u32[]{:S(2)}) copy-start(f32[56,64,64]{2,1,0:T(8,128)} %get-tuple-element.28.inner_ref) | copy-start | bytes 2752516
  77.4 1.0 %copy-start.9 = (f32[16,64,64]{2,1,0:T(8,128)S(1)}, f32[16,64,64]{2,1,0:T(8,128)}, u32[]{:S(2)}) copy-start(f32[16,64,64]{2,1,0:T(8,128)} %get-tuple-element.26.orth_ref) | copy-start | bytes 786436
  78.5 1.0 %copy-start.10 = (f32[16,64,64]{2,1,0:T(8,128)S(1)}, f32[16,64,64]{2,1,0:T(8,128)}, u32[]{:S(2)}) copy-start(f32[16,64,64]{2,1,0:T(8,128)} %get-tuple-element.27.leaf_ref) | copy-start | bytes 786436
  79.5 1.0 %copy-start.11 = (f32[16,64,64]{2,1,0:T(8,128)S(1)}, f32[16,64,64]{2,1,0:T(8,128)}, u32[]{:S(2)}) copy-start(f32[16,64,64]{2,1,0:T(8,128)} %get-tuple-element.25) | copy-start | bytes 786436

commit v3 on v2

--- a/solution.py
+++ b/solution.py
@@ -26,42 +26,9 @@
     return tn(e, nn(g, e))
 
 
-def local_tree(pos_ref, basis_ref, lt_ref, it_ref, gram_ref, img_ref, tmp):
-    blk = pos_ref[1]
-    for c in range(16):
-        b = basis_ref[c]
-        g = tn(b, b)
-        gram_ref[c] = g
-        tmp[c] = sandwich(lt_ref[c], g)
-    at, src = 16, 0
-    for count in (8, 4, 2, 1):
-        for n in range(count):
-            g = tmp[src + 2 * n] + tmp[src + 2 * n + 1]
-            gram_ref[at + n] = g
-            m = sandwich(it_ref[4 * count - 1 + count * blk + n], g)
-            if count == 1:
-                img_ref[...] = jnp.concatenate([g, m], axis=1)
-                gram_ref[31] = g
-            else:
-                tmp[src + 2 * count + n] = m
-        src += 2 * count
-        at += count
-
-
-def run_local_tree(pos, basis, lt, it):
-    vm = pl.BlockSpec(memory_space=pltpu.VMEM)
-    return pl.pallas_call(
-        local_tree,
-        out_shape=(jax.ShapeDtypeStruct((32, N, N), F32), jax.ShapeDtypeStruct((N, 2 * N), F32)),
-        in_specs=[pl.BlockSpec(memory_space=pltpu.SMEM), vm, vm, vm],
-        out_specs=(vm, vm),
-        scratch_shapes=[pltpu.VMEM((32, N, N), F32)],
-        compiler_params=pltpu.CompilerParams(vmem_limit_bytes=40 * 2**20),
-    )(pos, basis, lt, it)
-
-
 LANES = 128
 COPIES = 29
+VMEM = 60 * 2**20
 
 
 def eliminate(a_ref, w_ref):
@@ -126,12 +93,14 @@
 
     for p in range(8):
         panel(p)
-        targets = [(a_ref, jb, False) for jb in range(p + 1, 8)] + [(w_ref, jb, jb == p) for jb in range(p + 1)]
-
-        def step(ib, _):
-            trail(p, 8 * ib, targets)
-            return 0
-        lax.fori_loop(p + 1, 8, step, 0)
+        middle_block = (p + 9) // 2
+        for start, stop in ((p + 1, middle_block), (middle_block, 8)):
+            targets = [(a_ref, jb, False) for jb in range(start, 8)] + [(w_ref, jb, jb == p) for jb in range(p + 1)]
+
+            def step(ib, _):
+                trail(p, 8 * ib, targets)
+                return 0
+            lax.fori_loop(start, stop, step, 0)
 
 
 def factor_stack(g_ref, u_ref, w_ref, a, w, n):
@@ -149,23 +118,53 @@
     lax.fori_loop(0, N, save, 0, unroll=8)
 
 
-def lower_factors(g_ref, u_ref, w_ref, pack_ref, a, w):
-    factor_stack(g_ref, u_ref, w_ref, a, w, 32)
+def lower(pos_ref, basis_ref, lt_ref, it_ref, gm_ref, u_ref, w_ref, pack_ref, gram, tmp, e, a, w, sem):
+    blk = pos_ref[1]
+    fetches = []
+    for t, (count, at) in enumerate(((8, 0), (4, 8), (2, 12), (1, 14))):
+        c = pltpu.make_async_copy(it_ref.at[pl.ds(4 * count - 1 + count * blk, count)], e.at[pl.ds(at, count)], sem.at[t])
+        c.start()
+        fetches.append(c)
+
+    def keep(i, g):
+        gram[i * N:i * N + N, :] = g
+
+    for c in range(16):
+        b = basis_ref[c]
+        g = tn(b, b)
+        keep(c, g)
+        tmp[c] = sandwich(lt_ref[c], g)
+    at, src = 16, 0
+    for t, count in enumerate((8, 4, 2, 1)):
+        fetches[t].wait()
+        for n in range(count):
+            g = tmp[src + 2 * n] + tmp[src + 2 * n + 1]
+            keep(at + n, g)
+            m = sandwich(e[at - 16 + n], g)
+            if count == 1:
+                gm_ref[...] = jnp.concatenate([g, m], axis=1)
+                keep(31, g)
+            else:
+                tmp[src + 2 * count + n] = m
+        src += 2 * count
+        at += count
+    factor_stack(gram, u_ref, w_ref, a, w, 32)
     for c in range(8):
         pack_ref[c] = jnp.concatenate([u_ref[2 * c * N:2 * c * N + N, :], u_ref[2 * c * N + N:2 * c * N + 2 * N, :]], axis=1)
 
 
-def run_lower_factors(g):
+def run_lower(pos, basis, lt, it):
     vm = pl.BlockSpec(memory_space=pltpu.VMEM)
-    s = jax.ShapeDtypeStruct((32 * N, N), F32)
+    sd = jax.ShapeDtypeStruct
     return pl.pallas_call(
-        lower_factors,
-        out_shape=(s, s, jax.ShapeDtypeStruct((8, N, 2 * N), F32)),
-        in_specs=[vm],
-        out_specs=(vm, vm, vm),
-        scratch_shapes=[pltpu.VMEM((N, N, LANES), F32)] * 2,
-        compiler_params=pltpu.CompilerParams(vmem_limit_bytes=40 * 2**20),
-    )(g.reshape(32 * N, N))
+        lower,
+        out_shape=(sd((N, 2 * N), F32), sd((32 * N, N), F32), sd((32 * N, N), F32), sd((8, N, 2 * N), F32)),
+        in_specs=[pl.BlockSpec(memory_space=pltpu.SMEM), vm, vm, pl.BlockSpec(memory_space=pl.ANY)],
+        out_specs=(vm, vm, vm, vm),
+        scratch_shapes=[pltpu.VMEM((32 * N, N), F32), pltpu.VMEM((32, N, N), F32), pltpu.VMEM((15, N, N), F32)]
+        + [pltpu.VMEM((N, N, LANES), F32)] * 2 + [pltpu.SemaphoreType.DMA((4,))],
+        compiler_params=pltpu.CompilerParams(vmem_limit_bytes=VMEM),
+    )(pos, basis, lt, it)
 
 
 BF = jnp.bfloat16
@@ -181,8 +180,9 @@
     return h, l, pltpu.roll(h, N, 1), pltpu.roll(l, N, 1)
 
 
-def middle(table_ref, count_ref, gm_ref, pack_ref, u_ref, w_ref, basis_ref, lt_ref, it_ref, up_ref, c_ref,
-           orth_ref, newleaf_ref, g_ref, inner_ref, out_ref,
+def middle(table_ref, count_ref, gm_hbm, pack_hbm, u_hbm, w_hbm, basis_hbm, lt_hbm, it_hbm, up_hbm, c_ref,
+           orth_out, newleaf_out, g_ref, inner_out, out_ref,
+           pack_ref, u_ref, w_ref, basis_ref, lt_ref, it_ref, up_ref, orth_ref, newleaf_ref, inner_ref, fetch_sem,
            buf, s, r, cols, rows, all_u, all_t, quad, octet, four, send_sem, recv_sem, local_sem):
     leaf, blk = lax.axis_index("leaf"), lax.axis_index("blk")
     low, high = leaf % 8, leaf // 8
@@ -195,10 +195,16 @@
     barrier = pltpu.get_barrier_semaphore()
     for peer in peers:
         pl.semaphore_signal(barrier, inc=1, device_id=peer, device_id_type=pl.DeviceIdType.MESH)
+    fetches = {}
+    for i, (name, a, b) in enumerate((
+            ("gm", gm_hbm, quad.at[blk]), ("pack", pack_hbm, pack_ref), ("w", w_hbm, w_ref), ("basis", basis_hbm, basis_ref),
+            ("u", u_hbm, u_ref), ("lt", lt_hbm, lt_ref), ("it", it_hbm, it_ref), ("up", up_hbm, up_ref))):
+        fetches[name] = pltpu.make_async_copy(a, b, fetch_sem.at[i])
+        fetches[name].start()
+    own_u = pltpu.make_async_copy(pack_hbm, all_u.at[pl.ds((4 + blk) * 8, 8)], local_sem.at[1])
+    own_u.start()
     fetch = pltpu.make_async_copy(c_ref, buf, local_sem.at[0])
     fetch.start()
-    own_u = pltpu.make_async_copy(pack_ref, all_u.at[pl.ds((4 + blk) * 8, 8)], local_sem.at[1])
-    own_u.start()
     used = []
 
     def push(src, dst, peer):
@@ -222,19 +228,31 @@
     def orth(c):
         orth_ref[c] = nt(basis_ref[c], w(c))
 
-    for c in range(8):
-        orth(c)
-    quad[blk] = gm_ref[...]
+    fetches["gm"].wait()
+    fetches["pack"].wait()
     pl.semaphore_wait(barrier, len(peers))
 
     quads = [push(quad.at[blk], quad.at[blk], peer) for peer in (zup, zdown, zfar)]
     u_up = push(pack_ref, block(1, blk, 0, 8), zup)
     u_down = push(pack_ref, block(1, blk, 0, 8), zdown)
     sides = [push(pack_ref, block(0, blk, 0, 8), right), push(pack_ref, block(2, blk, 0, 8), left)]
-    for c in range(8, 16):
+    fetches["w"].wait()
+    fetches["basis"].wait()
+    for c in range(16):
         orth(c)
-    for c in range(16):
-        newleaf_ref[c] = nt(nn(u(c), lt_ref[c]), w(16 + c // 2))
+    fetches["u"].wait()
+    fetches["lt"].wait()
+    orth_store = pltpu.make_async_copy(orth_ref, orth_out, local_sem.at[6])
+    orth_store.start()
+    for c in range(8):
+        x = jnp.concatenate([nn(u(2 * c), lt_ref[2 * c]), nn(u(2 * c + 1), lt_ref[2 * c + 1])], axis=0)
+        x = nt(x, w(16 + c))
+        newleaf_ref[2 * c] = x[:N]
+        newleaf_ref[2 * c + 1] = x[N:]
+    leaf_store = pltpu.make_async_copy(newleaf_ref, newleaf_out, local_sem.at[7])
+    leaf_store.start()
+    fetches["it"].wait()
+    fetches["up"].wait()
 
     for c in quads:
         c.wait_recv()
@@ -260,9 +278,11 @@
 
     done, at = [], 16
     for count in (8, 4, 2):
-        for n in range(count):
-            e = it_ref[4 * count - 1 + count * blk + n]
-            done.append(nt(nn(u(at + n), e), w(at + count + n // 2)))
+        for n in range(0, count, 2):
+            first = 4 * count - 1 + count * blk + n
+            x = jnp.concatenate([nn(u(at + n), it_ref[first]), nn(u(at + n + 1), it_ref[first + 1])], axis=0)
+            x = nt(x, w(at + count + n // 2))
+            done += [x[:N], x[N:]]
         at += count
     for c in range(7):
         all_t[blk, c] = jnp.concatenate([done[2 * c], done[2 * c + 1]], axis=1)
@@ -372,9 +392,11 @@
             for n in range(count):
                 inner_ref[4 * count - 8 + count * b + n] = all_t[b, at // 2, :, at % 2 * N:at % 2 * N + N]
                 at += 1
+    inner_store = pltpu.make_async_copy(inner_ref, inner_out, local_sem.at[8])
+    inner_store.start()
     for c in used:
         c.wait_send()
-    for c in stores:
+    for c in stores + [orth_store, leaf_store, inner_store]:
         c.wait()
 
 
@@ -386,22 +408,29 @@
     return pl.pallas_call(
         middle,
         out_shape=(sd((16, N, N), F32), sd((16, N, N), F32), sd((16, N, N), F32), sd((56, N, N), F32), sd((N, N, 256), F32)),
-        in_specs=[sm, sm] + [vm] * 8 + [hbm],
-        out_specs=(vm, vm, vm, vm, hbm),
+        in_specs=[sm, sm] + [hbm] * 9,
+        out_specs=(hbm, hbm, vm, hbm, hbm),
         scratch_shapes=[
+            pltpu.VMEM((8, N, 2 * N), F32), pltpu.VMEM((32 * N, N), F32), pltpu.VMEM((32 * N, N), F32),
+            pltpu.VMEM((16, N, N), F32), pltpu.VMEM((16, N, N), F32), pltpu.VMEM((63, N, N), F32), pltpu.VMEM((31, N, N), F32),
+            pltpu.VMEM((16, N, N), F32), pltpu.VMEM((16, N, N), F32), pltpu.VMEM((56, N, N), F32), pltpu.SemaphoreType.DMA((8,)),
             pltpu.VMEM((N, N, 256), F32), pltpu.VMEM((128 * N, 2 * N), F32), pltpu.VMEM((128 * N, 2 * N), F32),
             pltpu.VMEM((192, N, 4 * N), BF), pltpu.VMEM((64, N, 2 * N), BF),
             pltpu.VMEM((96, N, 2 * N), F32), pltpu.VMEM((4, 7, N, 2 * N), F32),
             pltpu.VMEM((4, N, 2 * N), F32), pltpu.VMEM((8, N, N), F32), pltpu.VMEM((4, N, N), F32),
-            pltpu.SemaphoreType.DMA((COPIES,)), pltpu.SemaphoreType.DMA((COPIES,)), pltpu.SemaphoreType.DMA((6,)),
+            pltpu.SemaphoreType.DMA((COPIES,)), pltpu.SemaphoreType.DMA((COPIES,)), pltpu.SemaphoreType.DMA((9,)),
         ],
-        compiler_params=pltpu.CompilerParams(collective_id=0, has_side_effects=True, vmem_limit_bytes=58 * 2**20),
+        compiler_params=pltpu.CompilerParams(collective_id=0, has_side_effects=True, vmem_limit_bytes=VMEM),
     )(pairs.T, counts, gm, pack, u, w, basis, lt, it, up, jnp.transpose(coupling, (1, 2, 0)))
 
 
-def upper_factors(g_ref, it_ref, up_ref, pos_ref, orth_ref, leaf_ref, inner_ref, proj_ref,
-                  orth_out, leaf_out, inner_out, proj_out, upper_ref, a, w, u_all, w_all, head, sem):
+def upper_factors(g_ref, it_hbm, up_hbm, pos_ref, orth_ref, leaf_ref, inner_ref, proj_ref,
+                  orth_out, leaf_out, inner_out, proj_out, upper_ref, a, w, u_all, w_all, head, it_ref, up_ref, sem):
     leaf = pos_ref[0]
+    fetches = [pltpu.make_async_copy(it_hbm.at[pl.ds(0, 7)], it_ref, sem.at[8]),
+               pltpu.make_async_copy(up_hbm.at[pl.ds(jnp.maximum(leaf - 1, 0), 1)], up_ref, sem.at[9])]
+    for c in fetches:
+        c.start()
     copies = [pltpu.make_async_copy(orth_ref, orth_out, sem.at[0]), pltpu.make_async_copy(leaf_ref, leaf_out, sem.at[1]),
               pltpu.make_async_copy(inner_ref, inner_out.at[pl.ds(7, 56)], sem.at[2])]
     for q in range(4):
@@ -410,6 +439,8 @@
     for c in copies:
         c.start()
     factor_stack(g_ref, u_all, w_all, a, w, 16)
+    for c in fetches:
+        c.wait()
 
     def u(i):
         return u_all[pl.ds(i * N, N), :]
@@ -425,7 +456,7 @@
     last = pltpu.make_async_copy(head, inner_out.at[pl.ds(0, 7)], sem.at[7])
     last.start()
     level = jnp.where(leaf % 2 == 1, 1, jnp.where(leaf % 4 == 2, 2, jnp.where(leaf % 8 == 4, 3, jnp.where(leaf % 16 == 8, 4, 5))))
-    carried = nn(u(6 + level), up_ref[jnp.maximum(leaf - 1, 0)])
+    carried = nn(u(6 + level), up_ref[0])
     renewed = nt(carried, inverse(jnp.minimum(7 + level, 11)))
     upper_ref[0] = jnp.where(leaf == 0, u(11), jnp.where(leaf == 16, carried, renewed))
     for c in copies:
@@ -440,18 +471,17 @@
     return pl.pallas_call(
         upper_factors,
         out_shape=(sd((16, N, N), F32), sd((16, N, N), F32), sd((63, N, N), F32), sd((N, N, 256), F32), sd((1, N, N), F32)),
-        in_specs=[vm, vm, vm, pl.BlockSpec(memory_space=pltpu.SMEM)] + [hbm] * 4,
+        in_specs=[vm, hbm, hbm, pl.BlockSpec(memory_space=pltpu.SMEM)] + [hbm] * 4,
         out_specs=(hbm, hbm, hbm, hbm, vm),
         scratch_shapes=[pltpu.VMEM((N, N, LANES), F32)] * 2 + [pltpu.VMEM((16 * N, N), F32)] * 2 + [
-            pltpu.VMEM((7, N, N), F32), pltpu.SemaphoreType.DMA((8,))],
-        compiler_params=pltpu.CompilerParams(vmem_limit_bytes=40 * 2**20),
+            pltpu.VMEM((7, N, N), F32), pltpu.VMEM((7, N, N), F32), pltpu.VMEM((1, N, N), F32), pltpu.SemaphoreType.DMA((10,))],
+        compiler_params=pltpu.CompilerParams(vmem_limit_bytes=VMEM),
     )(g.reshape(16 * N, N), it, up, pos, orth, new_leaf, inner, proj)
 
 
 def body(leaf_basis, leaf_transfer, inner_transfer, upper_transfer, coupling, pairs, counts):
     pos = jnp.stack([lax.axis_index("leaf"), lax.axis_index("blk")]).astype(jnp.int32)
-    g1, gm = run_local_tree(pos, leaf_basis, leaf_transfer, inner_transfer)
-    u, w, pack = run_lower_factors(g1)
+    gm, u, w, pack = run_lower(pos, leaf_basis, leaf_transfer, inner_transfer)
     orth, new_leaf, g2, inner, proj = run_middle(
         pairs, counts, gm, pack, u, w, leaf_basis, leaf_transfer, inner_transfer, upper_transfer, coupling)
     orth, new_leaf, inner, proj, upper = run_upper_factors(

time: 92.8 us -> 284 us (3.06)
  Pallas kernels: 77.1 us -> 282 us
  local copies, waits for them, and re-layouts: 13.7 us -> 0 us
    pallas_call x1, Pallas kernels: 11.7 us -> 217 us  [run_upper_factors(): pl.pallas_call(upper_factors, out_shape=(sd((16, N, N), F32), sd((16, N,...]
    unnamed x28 -> x0, local copies, waits for them, and re-layouts: 13.7 us -> none
    pallas_call x2 -> x1, Pallas kernels: 15.4 us -> 17.3 us  [run_lower(): pl.pallas_call(lower, out_shape=(sd((N, 2 * N), F32), sd((32 * N, N), F32...]
where the time goes in v3:
time: 284 us
  Pallas kernels  282 us (99%)
    pallas_call x1, Pallas kernels, run_upper_factors(): pl.pallas_call(upper_factors, out_shape=(sd((16, N, N), F32), sd((16, N,...  217 us
    pallas_call x1, Pallas kernels, run_middle(): pl.pallas_call(middle, out_shape=(sd((16, N, N), F32), sd((16, N, N), F32...  47.6 us
    pallas_call x1, Pallas kernels, run_lower(): pl.pallas_call(lower, out_shape=(sd((N, 2 * N), F32), sd((32 * N, N), F32...  17.3 us

profile of v3, /device:TPU:1, one launch (start us, length us, event | category | flops | bytes accessed | tf_op | source)
XLA Modules:
  0.0 284.2 jit_solution(6649590275340959139)
XLA Ops:
  1.3 0.6 pad_add_fusion.pos_ref
  1.9 17.3 %shard_map.110 = (f32[64,128]{1,0:T(8,128)}, f32[2048,64]{1,0:T(8,128)}, f32[2048,64]{1,0:T(8,128)}, f32[8,64,128]{2,1,0:T(8,128)}) custom-call(s32[2]{0:T(128)} %pad_add_fusion.pos_ref, f32[16,64,64]{2,1,0:T(8,128)} %basis_hbm.1, f32[16,64,64]{2,1,0:T(8,128)} %lt_hbm.1, f32[63,64,64]{2,1,0:T(8,128)} %it_hbm.3), custom_call_target="tpu_custom_call" | custom-call | tf_op jit(solution)/shard_map/pallas_call | solution.py:159
  19.2 47.6 %shard_map.111 = (f32[16,64,64]{2,1,0:T(8,128)}, f32[16,64,64]{2,1,0:T(8,128)}, f32[16,64,64]{2,1,0:T(8,128)}, f32[56,64,64]{2,1,0:T(8,128)}, f32[64,64,256]{2,1,0:T(8,128)}) custom-call(s32[2,256]{1,0:T(2,128)} %bitcast.8, s32[1]{0:T(128)S(6)} %copy.12.count_ref, f32[64,128]{1,0:T(8,128)} %get-tuple-element.19.gm_hbm, ...), custom_call_target="tpu_custom_call" | custom-call | tf_op jit(solution)/shard_map/pallas_call | solution.py:408
  66.8 217.3 %shard_map.112 = (f32[16,64,64]{2,1,0:T(8,128)}, f32[16,64,64]{2,1,0:T(8,128)}, f32[63,64,64]{2,1,0:T(8,128)}, f32[64,64,256]{2,1,0:T(8,128)}, f32[1,64,64]{2,1,0:T(8,128)}) custom-call(f32[1024,64]{1,0:T(8,128)} %bitcast.7, f32[63,64,64]{2,1,0:T(8,128)} %it_hbm.3, f32[31,64,64]{2,1,0:T(8,128)} %up_hbm.3, s32[2]{0:T(128)} %pad_add_fusion.pos_ref, ...), custom_call_target="tpu_custom_call" | custom-call | tf_op jit(solution)/shard_map/pallas_call | solution.py:471

commit v4 on v3

v4 whole, which is shorter than its diff:
```python
import jax
import jax.numpy as jnp
from jax import lax
from jax.experimental import pallas as pl
from jax.experimental.pallas import tpu as pltpu
from jax.sharding import PartitionSpec as P

HIGH = lax.Precision.HIGHEST
F32 = jnp.float32
N = 64


def nn(a, b):
    return lax.dot_general(a, b, (((1,), (0,)), ((), ())), precision=HIGH, preferred_element_type=F32)


def tn(a, b):
    return lax.dot_general(a, b, (((0,), (0,)), ((), ())), precision=HIGH, preferred_element_type=F32)


def nt(a, b):
    return lax.dot_general(a, b, (((1,), (1,)), ((), ())), precision=HIGH, preferred_element_type=F32)


def sandwich(e, g):
    return tn(e, nn(g, e))


LANES = 128
COPIES = 29
VMEM = 60 * 2**20


def eliminate(a_ref, w_ref):
    sub = lax.broadcasted_iota(jnp.int32, (8, LANES), 0)

    def bc(x, i):
        return jnp.broadcast_to(x[i:i + 1, :], (8, LANES))

    def panel(p):
        k0 = 8 * p
        d = [a_ref[k0 + i, k0:k0 + 8, :] for i in range(8)]
        r, coef = [], {}
        for k in range(8):
            piv = bc(d[k], k)
            y = lax.rsqrt(piv)
            y = y * (1.5 - 0.5 * piv * y * y)
            r.append(y)
            d[k] = d[k] * y
            for i in range(k + 1, 8):
                coef[k, i] = bc(d[k], i)
                d[i] = d[i] - coef[k, i] * d[k]
        for i in range(8):
            a_ref[k0 + i, k0:k0 + 8, :] = d[i]

        def solve(x):
            for k in range(8):
                x[k] = x[k] * r[k]
                for i in range(k + 1, 8):
                    x[i] = x[i] - coef[k, i] * x[k]
            return x

        for jb in range(p + 1, 8):
            x = solve([a_ref[k0 + i, 8 * jb:8 * jb + 8, :] for i in range(8)])
            for i in range(8):
                a_ref[k0 + i, 8 * jb:8 * jb + 8, :] = x[i]
        for jb in range(p + 1):
            if jb < p:
                x = [w_ref[k0 + i, 8 * jb:8 * jb + 8, :] for i in range(8)]
            else:
                x = [jnp.where(sub == i, F32(1), F32(0)) for i in range(8)]
            x = solve(x)
            for i in range(8):
                w_ref[k0 + i, 8 * jb:8 * jb + 8, :] = x[i]

    def trail(p, row, targets):
        k0 = 8 * p
        for g in range(0, len(targets), 2):
            group = targets[g:g + 2]
            acc = {}
            for t, (ref, jb, fresh) in enumerate(group):
                for i in range(8):
                    acc[t, i] = jnp.zeros((8, LANES), F32) if fresh else ref[row + i, 8 * jb:8 * jb + 8, :]
            for k in range(8):
                pivots = [ref[k0 + k, 8 * jb:8 * jb + 8, :] for ref, jb, _ in group]
                for i in range(8):
                    c = jnp.broadcast_to(a_ref[k0 + k, pl.ds(row + i, 1), :], (8, LANES))
                    for t in range(len(group)):
                        acc[t, i] = acc[t, i] - c * pivots[t]
            for t, (ref, jb, _) in enumerate(group):
                for i in range(8):
                    ref[row + i, 8 * jb:8 * jb + 8, :] = acc[t, i]

    for p in range(8):
        panel(p)
        middle_block = (p + 9) // 2
        for start, stop in ((p + 1, middle_block), (middle_block, 8)):
            targets = [(a_ref, jb, False) for jb in range(start, 8)] + [(w_ref, jb, jb == p) for jb in range(p + 1)]

            def step(ib, _):
                trail(p, 8 * ib, targets)
                return 0
            lax.fori_loop(start, stop, step, 0)


def factor_stack(g_ref, uw_ref, a, w, n):
    def load(k, _):
        a[k] = jnp.concatenate([g_ref[pl.ds(k, n, stride=N), :]] * (LANES // n), axis=0).T
        return 0
    lax.fori_loop(0, N, load, 0, unroll=8)
    eliminate(a, w)
    col = lax.broadcasted_iota(jnp.int32, (N, LANES), 0)

    def save(k, _):
        x = jnp.concatenate([jnp.where(col >= k, a[k], F32(0)), jnp.where(col <= k, w[k], F32(0))], axis=0)
        uw_ref[pl.ds(k, n, stride=N), :] = x.T[:n]
        return 0
    lax.fori_loop(0, N, save, 0, unroll=8)


def lower(pos_ref, basis_ref, lt_ref, it_ref, gm_ref, pack_ref, tpack_ref, orth_ref, newleaf_ref, gram, tmp, e, a, winv, uw, sem):
    blk = pos_ref[1]
    fetches = []
    for t, (count, at) in enumerate(((8, 0), (4, 8), (2, 12), (1, 14))):
        c = pltpu.make_async_copy(it_ref.at[pl.ds(4 * count - 1 + count * blk, count)], e.at[pl.ds(at, count)], sem.at[t])
        c.start()
        fetches.append(c)

    def keep(i, g):
        gram[i * N:i * N + N, :] = g

    for c in range(16):
        b = basis_ref[c]
        g = tn(b, b)
        keep(c, g)
        tmp[c] = sandwich(lt_ref[c], g)
    at, src = 16, 0
    for t, count in enumerate((8, 4, 2, 1)):
        fetches[t].wait()
        for n in range(count):
            g = tmp[src + 2 * n] + tmp[src + 2 * n + 1]
            keep(at + n, g)
            m = sandwich(e[at - 16 + n], g)
            if count == 1:
                gm_ref[...] = jnp.concatenate([g, m], axis=1)
                keep(31, g)
            else:
                tmp[src + 2 * count + n] = m
        src += 2 * count
        at += count
    factor_stack(gram, uw, a, winv, 32)

    def u(i):
        return uw[i * N:i * N + N, 0:N]

    def w(i):
        return uw[i * N:i * N + N, N:2 * N]

    for c in range(8):
        pack_ref[c] = jnp.concatenate([u(2 * c), u(2 * c + 1)], axis=1)
    for c in range(16):
        orth_ref[c] = nt(basis_ref[c], w(c))
    for c in range(8):
        x = jnp.concatenate([nn(u(2 * c), lt_ref[2 * c]), nn(u(2 * c + 1), lt_ref[2 * c + 1])], axis=0)
        x = nt(x, w(16 + c))
        newleaf_ref[2 * c] = x[:N]
        newleaf_ref[2 * c + 1] = x[N:]
    at, pair = 16, 0
    for count in (8, 4, 2):
        for n in range(0, count, 2):
            x = jnp.concatenate([nn(u(at + n), e[at + n - 16]), nn(u(at + n + 1), e[at + n - 15])], axis=0)
            x = nt(x, w(at + count + n // 2))
            tpack_ref[pair] = jnp.concatenate([x[:N], x[N:]], axis=1)
            pair += 1
        at += count


def run_lower(pos, basis, lt, it):
    vm = pl.BlockSpec(memory_space=pltpu.VMEM)
    sd = jax.ShapeDtypeStruct
    return pl.pallas_call(
        lower,
        out_shape=(sd((N, 2 * N), F32), sd((8, N, 2 * N), F32), sd((7, N, 2 * N), F32), sd((16, N, N), F32), sd((16, N, N), F32)),
        in_specs=[pl.BlockSpec(memory_space=pltpu.SMEM), vm, vm, pl.BlockSpec(memory_space=pl.ANY)],
        out_specs=(vm,) * 5,
        scratch_shapes=[pltpu.VMEM((32 * N, N), F32), pltpu.VMEM((32, N, N), F32), pltpu.VMEM((15, N, N), F32)]
        + [pltpu.VMEM((N, N, LANES), F32)] * 2 + [pltpu.VMEM((32 * N, 2 * N), F32), pltpu.SemaphoreType.DMA((4,))],
        compiler_params=pltpu.CompilerParams(vmem_limit_bytes=VMEM),
    )(pos, basis, lt, it)


BF = jnp.bfloat16


def split(x):
    h = x.astype(BF).astype(F32)
    return h, (x - h).astype(BF).astype(F32)


def cut(x):
    h, l = split(x)
    return h, l, pltpu.roll(h, N, 1), pltpu.roll(l, N, 1)


def middle(gm_hbm, pack_hbm, tpack_hbm, it_hbm, up_hbm, u_out, t_out, head_ref, upper_ref,
           pack_ref, tpack_ref, it_ref, near_up, far_up, own_up, all_u, all_t, quad, octet, four, gram, a, winv, uw,
           send_sem, recv_sem, fetch_sem, store_sem):
    leaf, blk = lax.axis_index("leaf"), lax.axis_index("blk")
    low, high = leaf % 8, leaf // 8
    zup, zdown, zfar = [{"leaf": leaf, "blk": (blk + i) % 4} for i in (1, 3, 2)]
    right = {"leaf": (leaf + 1) % 32, "blk": blk}
    left = {"leaf": (leaf + 31) % 32, "blk": blk}
    mid = [{"leaf": high * 8 + (low + i) % 8, "blk": blk} for i in range(1, 8)]
    far = [{"leaf": (high + i) % 4 * 8 + low, "blk": blk} for i in range(1, 4)]
    peers = [zup, zdown, zfar, right, left] + mid + far
    barrier = pltpu.get_barrier_semaphore()
    for peer in peers:
        pl.semaphore_signal(barrier, inc=1, device_id=peer, device_id_type=pl.DeviceIdType.MESH)
    fetches = {}
    for i, (name, x, y) in enumerate((
            ("gm", gm_hbm, quad.at[blk]), ("pack", pack_hbm, pack_ref), ("it", it_hbm.at[pl.ds(0, 7)], it_ref),
            ("own", up_hbm.at[pl.ds(jnp.maximum(leaf - 1, 0), 1)], own_up), ("near", up_hbm.at[pl.ds(high * 8, 7)], near_up),
            ("far0", up_hbm.at[pl.ds(7, 1)], far_up.at[pl.ds(0, 1)]), ("far1", up_hbm.at[pl.ds(23, 1)], far_up.at[pl.ds(1, 1)]),
            ("tpack", tpack_hbm, tpack_ref))):
        fetches[name] = pltpu.make_async_copy(x, y, fetch_sem.at[i])
        fetches[name].start()
    used, stores = [], []

    def push(src, dst, peer):
        i = len(used)
        c = pltpu.make_async_remote_copy(
            src_ref=src, dst_ref=dst, send_sem=send_sem.at[i], recv_sem=recv_sem.at[i],
            device_id=peer, device_id_type=pl.DeviceIdType.MESH)
        c.start()
        used.append(c)
        return c

    def store(src, dst):
        c = pltpu.make_async_copy(src, dst, store_sem.at[len(stores)])
        c.start()
        stores.append(c)

    def block(d, b, start=0, count=8):
        return all_u.at[pl.ds((d * 4 + b) * 8 + start, count)]

    def keep(i, g):
        gram[i * N:i * N + N, :] = g

    fetches["gm"].wait()
    fetches["pack"].wait()
    pl.semaphore_wait(barrier, len(peers))
    quads = [push(quad.at[blk], quad.at[blk], peer) for peer in (zup, zdown, zfar)]
    u_up = push(pack_ref, block(1, blk), zup)
    u_down = push(pack_ref, block(1, blk), zdown)
    sides = [(push(pack_ref, block(0, blk), right), 0, blk), (push(pack_ref, block(2, blk), left), 2, blk)]
    fetches["tpack"].wait()
    store(pack_ref, u_out.at[pl.ds((4 + blk) * 8, 8)])
    store(tpack_ref, t_out.at[blk])

    fetches["it"].wait()
    for c in quads:
        c.wait_recv()
    root = None
    for n in range(2):
        keep(2 * n, quad[2 * n, :, 0:N])
        keep(2 * n + 1, quad[2 * n + 1, :, 0:N])
        g = quad[2 * n, :, N:2 * N] + quad[2 * n + 1, :, N:2 * N]
        keep(4 + n, g)
        m = sandwich(it_ref[1 + n], g)
        root = m if root is None else root + m
    keep(6, root)
    octet[low] = sandwich(it_ref[0], root)
    octets = [push(octet.at[low], octet.at[low], peer) for peer in mid]

    below, above, beyond = (blk + 3) % 4, (blk + 1) % 4, (blk + 2) % 4
    u_up.wait_recv()
    half_up = push(block(1, below, 0, 4), block(1, below, 0, 4), zup)
    u_down.wait_recv()
    half_down = push(block(1, above, 4, 4), block(1, above, 4, 4), zdown)
    for b in (below, above):
        sides += [(push(block(1, b), block(0, b), right), 0, b), (push(block(1, b), block(2, b), left), 2, b)]
        store(block(1, b), u_out.at[pl.ds((4 + b) * 8, 8)])

    for name in ("near", "far0", "far1", "own"):
        fetches[name].wait()
    for c in octets:
        c.wait_recv()
    first = [octet[2 * n] + octet[2 * n + 1] for n in range(4)]
    keep(7, octet[low // 2 * 2] + octet[low // 2 * 2 + 1])
    images = [sandwich(near_up[2 * n], first[n]) for n in range(4)]
    second = [images[2 * n] + images[2 * n + 1] for n in range(2)]
    keep(8, jnp.where(low < 4, second[0], second[1]))
    images = [sandwich(near_up[4 * n + 1], second[n]) for n in range(2)]
    third = images[0] + images[1]
    keep(9, third)
    four[high] = sandwich(near_up[3], third)
    fours = [push(four.at[high], four.at[high], peer) for peer in far]

    half_up.wait_recv()
    half_down.wait_recv()
    sides += [(push(block(1, beyond), block(0, beyond), right), 0, beyond), (push(block(1, beyond), block(2, beyond), left), 2, beyond)]
    store(block(1, beyond), u_out.at[pl.ds((4 + beyond) * 8, 8)])
    t_up = push(tpack_ref, all_t.at[blk], zup)
    t_down = push(tpack_ref, all_t.at[blk], zdown)

    for c in fours:
        c.wait_recv()
    fourth = [four[2 * n] + four[2 * n + 1] for n in range(2)]
    keep(10, jnp.where(high < 2, fourth[0], fourth[1]))
    images = [sandwich(far_up[n], fourth[n]) for n in range(2)]
    for n in range(11, 16):
        keep(n, images[0] + images[1])
    factor_stack(gram, uw, a, winv, 16)

    t_up.wait_recv()
    t_half_up = push(all_t.at[below, pl.ds(0, 4)], all_t.at[below, pl.ds(0, 4)], zup)
    t_down.wait_recv()
    t_half_down = push(all_t.at[above, pl.ds(4, 3)], all_t.at[above, pl.ds(4, 3)], zdown)
    for b in (below, above):
        store(all_t.at[b], t_out.at[b])

    def u(i):
        return uw[pl.ds(i * N, N), 0:N]

    def w(i):
        return uw[pl.ds(i * N, N), N:2 * N]

    head_ref[0] = nt(nn(u(6), it_ref[0]), w(7))
    for n in range(2):
        head_ref[1 + n] = nt(nn(u(4 + n), it_ref[1 + n]), w(6))
    for n in range(4):
        head_ref[3 + n] = nt(nn(u(n), it_ref[3 + n]), w(4 + n // 2))
    level = jnp.where(leaf % 2 == 1, 1, jnp.where(leaf % 4 == 2, 2, jnp.where(leaf % 8 == 4, 3, jnp.where(leaf % 16 == 8, 4, 5))))
    carried = nn(u(6 + level), own_up[0])
    renewed = nt(carried, w(jnp.minimum(7 + level, 11)))
    upper_ref[0] = jnp.where(leaf == 0, u(11), jnp.where(leaf == 16, carried, renewed))

    for c, d, b in sides:
        c.wait_recv()
        store(block(d, b), u_out.at[pl.ds((d * 4 + b) * 8, 8)])
    t_half_up.wait_recv()
    t_half_down.wait_recv()
    store(all_t.at[beyond], t_out.at[beyond])
    for c in used:
        c.wait_send()
    for c in stores:
        c.wait()


def run_middle(gm, pack, tpack, it, up):
    vm = pl.BlockSpec(memory_space=pltpu.VMEM)
    hbm = pl.BlockSpec(memory_space=pl.ANY)
    sd = jax.ShapeDtypeStruct
    return pl.pallas_call(
        middle,
        out_shape=(sd((96, N, 2 * N), F32), sd((4, 7, N, 2 * N), F32), sd((7, N, N), F32), sd((1, N, N), F32)),
        in_specs=[hbm] * 5,
        out_specs=(hbm, hbm, vm, vm),
        scratch_shapes=[
            pltpu.VMEM((8, N, 2 * N), F32), pltpu.VMEM((7, N, 2 * N), F32), pltpu.VMEM((7, N, N), F32),
            pltpu.VMEM((7, N, N), F32), pltpu.VMEM((2, N, N), F32), pltpu.VMEM((1, N, N), F32),
            pltpu.VMEM((96, N, 2 * N), F32), pltpu.VMEM((4, 7, N, 2 * N), F32),
            pltpu.VMEM((4, N, 2 * N), F32), pltpu.VMEM((8, N, N), F32), pltpu.VMEM((4, N, N), F32),
            pltpu.VMEM((16 * N, N), F32), pltpu.VMEM((N, N, LANES), F32), pltpu.VMEM((N, N, LANES), F32),
            pltpu.VMEM((16 * N, 2 * N), F32),
            pltpu.SemaphoreType.DMA((COPIES,)), pltpu.SemaphoreType.DMA((COPIES,)), pltpu.SemaphoreType.DMA((8,)),
            pltpu.SemaphoreType.DMA((16,)),
        ],
        compiler_params=pltpu.CompilerParams(collective_id=0, has_side_effects=True, vmem_limit_bytes=VMEM),
    )(gm, pack, tpack, it, up)


def project(table_ref, count_ref, pos_ref, c_ref, u_hbm, t_hbm, head_hbm, inner_out, out_ref,
            buf, s, r, cols, rows, all_u, all_t, inner_ref, fetch_sem, store_sem):
    fetches = []
    for q in range(4):
        part = pl.ds(16 * q, 16)
        fetches.append(pltpu.make_async_copy(c_ref.at[part], buf.at[part], fetch_sem.at[q]))
    fetches.append(pltpu.make_async_copy(u_hbm, all_u, fetch_sem.at[4]))
    fetches.append(pltpu.make_async_copy(t_hbm, all_t, fetch_sem.at[5]))
    fetches.append(pltpu.make_async_copy(head_hbm, inner_ref.at[pl.ds(0, 7)], fetch_sem.at[6]))
    for c in fetches:
        c.start()
    lane = lax.broadcasted_iota(jnp.int32, (N, 2 * N), 1)
    lower_lanes = lane < N

    def turn(k, _):
        x = jnp.concatenate([buf[k, :, 0:128], buf[k, :, 128:256]], axis=0)
        s[pl.ds(k, 128, stride=N), :] = x.T
        return 0
    for q in range(4):
        fetches[q].wait()
        lax.fori_loop(16 * q, 16 * q + 16, turn, 0, unroll=8)

    def prepare(p, _):
        h, l, hr, lr = cut(all_u[p])
        cols[2 * p] = jnp.concatenate([jnp.where(lower_lanes, h, hr), jnp.where(lower_lanes, l, lr)], axis=1).astype(BF)
        cols[2 * p + 1] = jnp.concatenate([jnp.where(lower_lanes, hr, h), jnp.where(lower_lanes, lr, l)], axis=1).astype(BF)
        return 0

    def prepare_rows(p, _):
        h, l, hr, lr = cut(all_u[32 + p])
        rows[2 * p] = jnp.where(lower_lanes, h, lr).astype(BF)
        rows[2 * p + 1] = jnp.where(lower_lanes, hr, l).astype(BF)
        return 0
    fetches[4].wait()
    lax.fori_loop(0, 96, prepare, 0, unroll=8)
    lax.fori_loop(0, 32, prepare_rows, 0, unroll=8)

    fetches[5].wait()
    fetches[6].wait()
    for b in range(4):
        at = 0
        for count in (8, 4, 2):
            for n in range(count):
                inner_ref[4 * count - 1 + count * b + n] = all_t[b, at // 2, :, at % 2 * N:at % 2 * N + N]
                at += 1
    stores = [pltpu.make_async_copy(inner_ref, inner_out, store_sem.at[4])]
    stores[0].start()
    base = pos_ref[0] * 64

    def slot(k, d):
        i = jnp.clip(table_ref[0, k] - base, 0, 63)
        j = jnp.clip(table_ref[1, k] - base + 64, 0, 191)
        d = d.astype(BF)
        y = lax.dot_general(jnp.concatenate([d, d], axis=1), cols[j], (((1,), (1,)), ((), ())), preferred_element_type=F32)
        h = y.astype(BF)
        l = (y - h.astype(F32)).astype(BF)
        x = rows[i]
        return lax.dot_general(jnp.concatenate([x, x], axis=1), jnp.concatenate([h, h, l, l], axis=0),
                               (((1,), (0,)), ((), ())), preferred_element_type=F32)

    def both(k, _):
        at = pl.ds(pl.multiple_of(k * N, N), N)
        h, l, hr, lr = cut(s[at, :])
        r[at, :] = jnp.concatenate([slot(k, jnp.where(lower_lanes, h, lr)), slot(k + 128, jnp.where(lower_lanes, hr, l))], axis=1)
        return 0
    lax.fori_loop(0, 128, both, 0, unroll=32)

    live = count_ref[0]

    def back(k, _):
        x = r[pl.ds(k, 128, stride=N), :].T
        buf[k, :, 0:128] = jnp.where(lane < live, x[:N], F32(0))
        buf[k, :, 128:256] = jnp.where(lane + 128 < live, x[N:], F32(0))
        return 0
    for q in range(4):
        lax.fori_loop(16 * q, 16 * q + 16, back, 0, unroll=8)
        part = pl.ds(16 * q, 16)
        c = pltpu.make_async_copy(buf.at[part], out_ref.at[part], store_sem.at[q])
        c.start()
        stores.append(c)
    for c in stores:
        c.wait()


def run_project(pairs, counts, pos, coupling, u, t, head):
    sm = pl.BlockSpec(memory_space=pltpu.SMEM)
    hbm = pl.BlockSpec(memory_space=pl.ANY)
    sd = jax.ShapeDtypeStruct
    inner, out = pl.pallas_call(
        project,
        out_shape=(sd((63, N, N), F32), sd((N, N, 256), F32)),
        in_specs=[sm, sm, sm, hbm, hbm, hbm, hbm],
        out_specs=(hbm, hbm),
        scratch_shapes=[
            pltpu.VMEM((N, N, 256), F32), pltpu.VMEM((128 * N, 2 * N), F32), pltpu.VMEM((128 * N, 2 * N), F32),
            pltpu.VMEM((192, N, 4 * N), BF), pltpu.VMEM((64, N, 2 * N), BF),
            pltpu.VMEM((96, N, 2 * N), F32), pltpu.VMEM((4, 7, N, 2 * N), F32), pltpu.VMEM((63, N, N), F32),
            pltpu.SemaphoreType.DMA((7,)), pltpu.SemaphoreType.DMA((5,)),
        ],
        compiler_params=pltpu.CompilerParams(vmem_limit_bytes=VMEM),
    )(pairs.T, counts, pos, jnp.transpose(coupling, (1, 2, 0)), u, t, head)
    return inner, jnp.transpose(out, (2, 0, 1))


def body(leaf_basis, leaf_transfer, inner_transfer, upper_transfer, coupling, pairs, counts):
    pos = jnp.stack([lax.axis_index("leaf"), lax.axis_index("blk")]).astype(jnp.int32)
    gm, pack, tpack, orth, new_leaf = run_lower(pos, leaf_basis, leaf_transfer, inner_transfer)
    all_u, all_t, head, upper = run_middle(gm, pack, tpack, inner_transfer, upper_transfer)
    inner, out = run_project(pairs, counts, pos, coupling, all_u, all_t, head)
    return orth, new_leaf, inner, upper, out


def solution(mesh):
    in_specs = (
        P(("leaf", "blk"), None, None),
        P(("leaf", "blk"), None, None),
        P("leaf", None, None),
        P(),
        P(("leaf", "blk"), None, None),
        P(("leaf", "blk"), None),
        P(("leaf", "blk")),
    )
    out_specs = (
        P(("leaf", "blk"), None, None),
        P(("leaf", "blk"), None, None),
        P("leaf", None, None),
        P("leaf", None, None),
        P(("leaf", "blk"), None, None),
    )
    return jax.shard_map(body, mesh=mesh, in_specs=in_specs, out_specs=out_specs, check_vma=False)
```

time: 284 us -> 84.2 us (0.30)
  Pallas kernels: 282 us -> 81.5 us
    pallas_call x3, Pallas kernels: 282 us -> 81.5 us  [the longest x1 44.7 us: run_middle(): pl.pallas_call(middle, out_shape=(sd((96, N, 2 * N), F32), sd((4, 7, N, 2...]
where the time goes in v4:
time: 84.2 us; the launch traced here: 84 us
  Pallas kernels  81.5 us (97%)
  between operations  1.32 us (2%)
    pallas_call x1, Pallas kernels, run_middle(): pl.pallas_call(middle, out_shape=(sd((96, N, 2 * N), F32), sd((4, 7, N, 2...  44.7 us
    pallas_call x1, Pallas kernels, run_lower(): pl.pallas_call(lower, out_shape=(sd((N, 2 * N), F32), sd((8, N, 2 * N), F...  18.7 us
    pallas_call x1, Pallas kernels, run_project(): pl.pallas_call(project, out_shape=(sd((63, N, N), F32), sd((N, N, 256), F...  18.1 us

profile of v4, /device:TPU:1, one launch (start us, length us, event | category | flops | bytes accessed | tf_op | source)
XLA Modules:
  0.0 84.0 jit_solution(13791818267221994574)
XLA Ops:
  1.3 0.6 pad_add_fusion.pos_ref
  1.9 18.7 %shard_map.110 = (f32[64,128]{1,0:T(8,128)}, f32[8,64,128]{2,1,0:T(8,128)}, f32[7,64,128]{2,1,0:T(8,128)}, f32[16,64,64]{2,1,0:T(8,128)}, f32[16,64,64]{2,1,0:T(8,128)}) custom-call(s32[2]{0:T(128)} %pad_add_fusion.pos_ref, f32[16,64,64]{2,1,0:T(8,128)} %basis_ref.1, f32[16,64,64]{2,1,0:T(8,128)} %lt_ref.1, f32[63,64,64]{2,1,0:T(8,128)} %it_hbm.1), custom_call_target="tpu_custom_call" | custom-call | tf_op jit(solution)/shard_map/pallas_call | solution.py:181
  20.6 44.7 %shard_map.111 = (f32[96,64,128]{2,1,0:T(8,128)}, f32[4,7,64,128]{3,2,1,0:T(8,128)}, f32[7,64,64]{2,1,0:T(8,128)}, f32[1,64,64]{2,1,0:T(8,128)}) custom-call(f32[64,128]{1,0:T(8,128)} %get-tuple-element.18.gm_hbm, f32[8,64,128]{2,1,0:T(8,128)} %get-tuple-element.19.pack_hbm, f32[7,64,128]{2,1,0:T(8,128)} %get-tuple-element.20.tpack_hbm, ...), custom_call_target="tpu_custom_call" | custom-call | tf_op jit(solution)/shard_map/pallas_call | solution.py:354
  65.3 0.0 copy-start
  65.3 18.1 %shard_map.112 = (f32[63,64,64]{2,1,0:T(8,128)}, f32[64,64,256]{2,1,0:T(8,128)}) custom-call(s32[2,256]{1,0:T(2,128)} %bitcast.6, s32[1]{0:T(128)S(6)} %copy.13.count_ref, s32[2]{0:T(128)} %pad_add_fusion.pos_ref, f32[64,64,256]{2,1,0:T(8,128)} %bitcast.5, f32[96,64,128]{2,1,0:T(8,128)} %get-tuple-element.21.u_hbm, ...), custom_call_target="tpu_custom_call" | custom-call | tf_op jit(solution)/shard_map/pallas_call | solution.py:461
  83.4 0.0 copy-done
  83.4 0.6 copy.14
Async XLA Ops:
  65.3 18.1 %copy-start = (f32[1,64,64]{2,1,0:T(8,128)S(1)}, f32[1,64,64]{2,1,0:T(8,128)}, u32[]{:S(2)}) copy-start(f32[1,64,64]{2,1,0:T(8,128)} %get-tuple-element.35) | copy-start | bytes 49156

commit v5 on v4

--- a/solution.py
+++ b/solution.py
@@ -103,12 +103,16 @@
             lax.fori_loop(start, stop, step, 0)
 
 
-def factor_stack(g_ref, uw_ref, a, w, n):
+def factor_stack(g_ref, uw_ref, a, w, n, loaded=None, eliminated=None):
     def load(k, _):
         a[k] = jnp.concatenate([g_ref[pl.ds(k, n, stride=N), :]] * (LANES // n), axis=0).T
         return 0
     lax.fori_loop(0, N, load, 0, unroll=8)
+    if loaded is not None:
+        loaded()
     eliminate(a, w)
+    if eliminated is not None:
+        eliminated()
     col = lax.broadcasted_iota(jnp.int32, (N, LANES), 0)
 
     def save(k, _):
@@ -118,77 +122,6 @@
     lax.fori_loop(0, N, save, 0, unroll=8)
 
 
-def lower(pos_ref, basis_ref, lt_ref, it_ref, gm_ref, pack_ref, tpack_ref, orth_ref, newleaf_ref, gram, tmp, e, a, winv, uw, sem):
-    blk = pos_ref[1]
-    fetches = []
-    for t, (count, at) in enumerate(((8, 0), (4, 8), (2, 12), (1, 14))):
-        c = pltpu.make_async_copy(it_ref.at[pl.ds(4 * count - 1 + count * blk, count)], e.at[pl.ds(at, count)], sem.at[t])
-        c.start()
-        fetches.append(c)
-
-    def keep(i, g):
-        gram[i * N:i * N + N, :] = g
-
-    for c in range(16):
-        b = basis_ref[c]
-        g = tn(b, b)
-        keep(c, g)
-        tmp[c] = sandwich(lt_ref[c], g)
-    at, src = 16, 0
-    for t, count in enumerate((8, 4, 2, 1)):
-        fetches[t].wait()
-        for n in range(count):
-            g = tmp[src + 2 * n] + tmp[src + 2 * n + 1]
-            keep(at + n, g)
-            m = sandwich(e[at - 16 + n], g)
-            if count == 1:
-                gm_ref[...] = jnp.concatenate([g, m], axis=1)
-                keep(31, g)
-            else:
-                tmp[src + 2 * count + n] = m
-        src += 2 * count
-        at += count
-    factor_stack(gram, uw, a, winv, 32)
-
-    def u(i):
-        return uw[i * N:i * N + N, 0:N]
-
-    def w(i):
-        return uw[i * N:i * N + N, N:2 * N]
-
-    for c in range(8):
-        pack_ref[c] = jnp.concatenate([u(2 * c), u(2 * c + 1)], axis=1)
-    for c in range(16):
-        orth_ref[c] = nt(basis_ref[c], w(c))
-    for c in range(8):
-        x = jnp.concatenate([nn(u(2 * c), lt_ref[2 * c]), nn(u(2 * c + 1), lt_ref[2 * c + 1])], axis=0)
-        x = nt(x, w(16 + c))
-        newleaf_ref[2 * c] = x[:N]
-        newleaf_ref[2 * c + 1] = x[N:]
-    at, pair = 16, 0
-    for count in (8, 4, 2):
-        for n in range(0, count, 2):
-            x = jnp.concatenate([nn(u(at + n), e[at + n - 16]), nn(u(at + n + 1), e[at + n - 15])], axis=0)
-            x = nt(x, w(at + count + n // 2))
-            tpack_ref[pair] = jnp.concatenate([x[:N], x[N:]], axis=1)
-            pair += 1
-        at += count
-
-
-def run_lower(pos, basis, lt, it):
-    vm = pl.BlockSpec(memory_space=pltpu.VMEM)
-    sd = jax.ShapeDtypeStruct
-    return pl.pallas_call(
-        lower,
-        out_shape=(sd((N, 2 * N), F32), sd((8, N, 2 * N), F32), sd((7, N, 2 * N), F32), sd((16, N, N), F32), sd((16, N, N), F32)),
-        in_specs=[pl.BlockSpec(memory_space=pltpu.SMEM), vm, vm, pl.BlockSpec(memory_space=pl.ANY)],
-        out_specs=(vm,) * 5,
-        scratch_shapes=[pltpu.VMEM((32 * N, N), F32), pltpu.VMEM((32, N, N), F32), pltpu.VMEM((15, N, N), F32)]
-        + [pltpu.VMEM((N, N, LANES), F32)] * 2 + [pltpu.VMEM((32 * N, 2 * N), F32), pltpu.SemaphoreType.DMA((4,))],
-        compiler_params=pltpu.CompilerParams(vmem_limit_bytes=VMEM),
-    )(pos, basis, lt, it)
-
-
 BF = jnp.bfloat16
 
 
@@ -202,8 +135,8 @@
     return h, l, pltpu.roll(h, N, 1), pltpu.roll(l, N, 1)
 
 
-def middle(gm_hbm, pack_hbm, tpack_hbm, it_hbm, up_hbm, u_out, t_out, head_ref, upper_ref,
-           pack_ref, tpack_ref, it_ref, near_up, far_up, own_up, all_u, all_t, quad, octet, four, gram, a, winv, uw,
+def tree(basis_hbm, lt_hbm, it_hbm, up_hbm, orth_out, newleaf_out, u_out, t_out, head_ref, upper_ref,
+         basis_ref, lt_ref, e, tmp, orth_ref, newleaf_ref, gram_low, uw_low, pack_ref, tpack_ref, it_ref, near_up, far_up, own_up, all_u, all_t, quad, octet, four, gram, a, winv, uw,
            send_sem, recv_sem, fetch_sem, store_sem):
     leaf, blk = lax.axis_index("leaf"), lax.axis_index("blk")
     low, high = leaf % 8, leaf // 8
@@ -217,11 +150,14 @@
     for peer in peers:
         pl.semaphore_signal(barrier, inc=1, device_id=peer, device_id_type=pl.DeviceIdType.MESH)
     fetches = {}
-    for i, (name, x, y) in enumerate((
-            ("gm", gm_hbm, quad.at[blk]), ("pack", pack_hbm, pack_ref), ("it", it_hbm.at[pl.ds(0, 7)], it_ref),
-            ("own", up_hbm.at[pl.ds(jnp.maximum(leaf - 1, 0), 1)], own_up), ("near", up_hbm.at[pl.ds(high * 8, 7)], near_up),
-            ("far0", up_hbm.at[pl.ds(7, 1)], far_up.at[pl.ds(0, 1)]), ("far1", up_hbm.at[pl.ds(23, 1)], far_up.at[pl.ds(1, 1)]),
-            ("tpack", tpack_hbm, tpack_ref))):
+    wanted = [("basis", basis_hbm, basis_ref), ("lt", lt_hbm, lt_ref)]
+    for count, at in ((8, 0), (4, 8), (2, 12), (1, 14)):
+        wanted.append(("e%d" % count, it_hbm.at[pl.ds(4 * count - 1 + count * blk, count)], e.at[pl.ds(at, count)]))
+    wanted += [
+        ("it", it_hbm.at[pl.ds(0, 7)], it_ref), ("own", up_hbm.at[pl.ds(jnp.maximum(leaf - 1, 0), 1)], own_up),
+        ("near", up_hbm.at[pl.ds(high * 8, 7)], near_up), ("far0", up_hbm.at[pl.ds(7, 1)], far_up.at[pl.ds(0, 1)]),
+        ("far1", up_hbm.at[pl.ds(23, 1)], far_up.at[pl.ds(1, 1)])]
+    for i, (name, x, y) in enumerate(wanted):
         fetches[name] = pltpu.make_async_copy(x, y, fetch_sem.at[i])
         fetches[name].start()
     used, stores = [], []
@@ -246,40 +182,71 @@
     def keep(i, g):
         gram[i * N:i * N + N, :] = g
 
-    fetches["gm"].wait()
-    fetches["pack"].wait()
+    fetches["basis"].wait()
+    fetches["lt"].wait()
+    for c in range(16):
+        b = basis_ref[c]
+        g = tn(b, b)
+        gram_low[c * N:c * N + N, :] = g
+        tmp[c] = sandwich(lt_ref[c], g)
+    at, done = 16, 0
+    for count in (8, 4, 2, 1):
+        fetches["e%d" % count].wait()
+        for n in range(count):
+            g = tmp[done + 2 * n] + tmp[done + 2 * n + 1]
+            gram_low[(at + n) * N:(at + n) * N + N, :] = g
+            m = sandwich(e[at - 16 + n], g)
+            if count == 1:
+                quad[blk] = jnp.concatenate([g, m], axis=1)
+                gram_low[31 * N:32 * N, :] = g
+            else:
+                tmp[done + 2 * count + n] = m
+        done += 2 * count
+        at += count
     pl.semaphore_wait(barrier, len(peers))
     quads = [push(quad.at[blk], quad.at[blk], peer) for peer in (zup, zdown, zfar)]
+    octets = []
+
+    def subtree_top():
+        fetches["it"].wait()
+        for c in quads:
+            c.wait_recv()
+        root = None
+        for n in range(2):
+            keep(2 * n, quad[2 * n, :, 0:N])
+            keep(2 * n + 1, quad[2 * n + 1, :, 0:N])
+            g = quad[2 * n, :, N:2 * N] + quad[2 * n + 1, :, N:2 * N]
+            keep(4 + n, g)
+            m = sandwich(it_ref[1 + n], g)
+            root = m if root is None else root + m
+        keep(6, root)
+        octet[low] = sandwich(it_ref[0], root)
+        octets.extend([push(octet.at[low], octet.at[low], peer) for peer in mid])
+
+    factor_stack(gram_low, uw_low, a, winv, 32, eliminated=subtree_top)
+
+    def u_low(i):
+        return uw_low[i * N:i * N + N, 0:N]
+
+    def w_low(i):
+        return uw_low[i * N:i * N + N, N:2 * N]
+
+    for c in range(8):
+        pack_ref[c] = jnp.concatenate([u_low(2 * c), u_low(2 * c + 1)], axis=1)
     u_up = push(pack_ref, block(1, blk), zup)
     u_down = push(pack_ref, block(1, blk), zdown)
     sides = [(push(pack_ref, block(0, blk), right), 0, blk), (push(pack_ref, block(2, blk), left), 2, blk)]
-    fetches["tpack"].wait()
     store(pack_ref, u_out.at[pl.ds((4 + blk) * 8, 8)])
-    store(tpack_ref, t_out.at[blk])
-
-    fetches["it"].wait()
-    for c in quads:
-        c.wait_recv()
-    root = None
-    for n in range(2):
-        keep(2 * n, quad[2 * n, :, 0:N])
-        keep(2 * n + 1, quad[2 * n + 1, :, 0:N])
-        g = quad[2 * n, :, N:2 * N] + quad[2 * n + 1, :, N:2 * N]
-        keep(4 + n, g)
-        m = sandwich(it_ref[1 + n], g)
-        root = m if root is None else root + m
-    keep(6, root)
-    octet[low] = sandwich(it_ref[0], root)
-    octets = [push(octet.at[low], octet.at[low], peer) for peer in mid]
-
-    below, above, beyond = (blk + 3) % 4, (blk + 1) % 4, (blk + 2) % 4
-    u_up.wait_recv()
-    half_up = push(block(1, below, 0, 4), block(1, below, 0, 4), zup)
-    u_down.wait_recv()
-    half_down = push(block(1, above, 4, 4), block(1, above, 4, 4), zdown)
-    for b in (below, above):
-        sides += [(push(block(1, b), block(0, b), right), 0, b), (push(block(1, b), block(2, b), left), 2, b)]
-        store(block(1, b), u_out.at[pl.ds((4 + b) * 8, 8)])
+
+    for c in range(16):
+        orth_ref[c] = nt(basis_ref[c], w_low(c))
+    store(orth_ref, orth_out)
+    for c in range(8):
+        x = jnp.concatenate([nn(u_low(2 * c), lt_ref[2 * c]), nn(u_low(2 * c + 1), lt_ref[2 * c + 1])], axis=0)
+        x = nt(x, w_low(16 + c))
+        newleaf_ref[2 * c] = x[:N]
+        newleaf_ref[2 * c + 1] = x[N:]
+    store(newleaf_ref, newleaf_out)
 
     for name in ("near", "far0", "far1", "own"):
         fetches[name].wait()
@@ -296,10 +263,24 @@
     four[high] = sandwich(near_up[3], third)
     fours = [push(four.at[high], four.at[high], peer) for peer in far]
 
-    half_up.wait_recv()
-    half_down.wait_recv()
-    sides += [(push(block(1, beyond), block(0, beyond), right), 0, beyond), (push(block(1, beyond), block(2, beyond), left), 2, beyond)]
-    store(block(1, beyond), u_out.at[pl.ds((4 + beyond) * 8, 8)])
+    below, above, beyond = (blk + 3) % 4, (blk + 1) % 4, (blk + 2) % 4
+    u_up.wait_recv()
+    half_up = push(block(1, below, 0, 4), block(1, below, 0, 4), zup)
+    u_down.wait_recv()
+    half_down = push(block(1, above, 4, 4), block(1, above, 4, 4), zdown)
+    for b in (below, above):
+        sides += [(push(block(1, b), block(0, b), right), 0, b), (push(block(1, b), block(2, b), left), 2, b)]
+        store(block(1, b), u_out.at[pl.ds((4 + b) * 8, 8)])
+
+    at, pair = 16, 0
+    for count in (8, 4, 2):
+        for n in range(0, count, 2):
+            x = jnp.concatenate([nn(u_low(at + n), e[at + n - 16]), nn(u_low(at + n + 1), e[at + n - 15])], axis=0)
+            x = nt(x, w_low(at + count + n // 2))
+            tpack_ref[pair] = jnp.concatenate([x[:N], x[N:]], axis=1)
+            pair += 1
+        at += count
+    store(tpack_ref, t_out.at[blk])
     t_up = push(tpack_ref, all_t.at[blk], zup)
     t_down = push(tpack_ref, all_t.at[blk], zdown)
 
@@ -310,7 +291,14 @@
     images = [sandwich(far_up[n], fourth[n]) for n in range(2)]
     for n in range(11, 16):
         keep(n, images[0] + images[1])
-    factor_stack(gram, uw, a, winv, 16)
+
+    def opposite():
+        half_up.wait_recv()
+        half_down.wait_recv()
+        sides.extend([(push(block(1, beyond), block(0, beyond), right), 0, beyond), (push(block(1, beyond), block(2, beyond), left), 2, beyond)])
+        store(block(1, beyond), u_out.at[pl.ds((4 + beyond) * 8, 8)])
+
+    factor_stack(gram, uw, a, winv, 16, loaded=opposite)
 
     t_up.wait_recv()
     t_half_up = push(all_t.at[below, pl.ds(0, 4)], all_t.at[below, pl.ds(0, 4)], zup)
@@ -347,30 +335,35 @@
         c.wait()
 
 
-def run_middle(gm, pack, tpack, it, up):
+def run_tree(basis, lt, it, up):
     vm = pl.BlockSpec(memory_space=pltpu.VMEM)
     hbm = pl.BlockSpec(memory_space=pl.ANY)
     sd = jax.ShapeDtypeStruct
+    leaves = pltpu.VMEM((16, N, N), F32)
+    lanes = pltpu.VMEM((N, N, LANES), F32)
     return pl.pallas_call(
-        middle,
-        out_shape=(sd((96, N, 2 * N), F32), sd((4, 7, N, 2 * N), F32), sd((7, N, N), F32), sd((1, N, N), F32)),
-        in_specs=[hbm] * 5,
-        out_specs=(hbm, hbm, vm, vm),
+        tree,
+        out_shape=(sd((16, N, N), F32), sd((16, N, N), F32), sd((96, N, 2 * N), F32), sd((4, 7, N, 2 * N), F32),
+                   sd((7, N, N), F32), sd((1, N, N), F32)),
+        in_specs=[hbm] * 4,
+        out_specs=(hbm, hbm, hbm, hbm, vm, vm),
         scratch_shapes=[
+            leaves, leaves, pltpu.VMEM((15, N, N), F32), pltpu.VMEM((32, N, N), F32), leaves, leaves,
+            pltpu.VMEM((32 * N, N), F32), pltpu.VMEM((32 * N, 2 * N), F32),
             pltpu.VMEM((8, N, 2 * N), F32), pltpu.VMEM((7, N, 2 * N), F32), pltpu.VMEM((7, N, N), F32),
             pltpu.VMEM((7, N, N), F32), pltpu.VMEM((2, N, N), F32), pltpu.VMEM((1, N, N), F32),
             pltpu.VMEM((96, N, 2 * N), F32), pltpu.VMEM((4, 7, N, 2 * N), F32),
             pltpu.VMEM((4, N, 2 * N), F32), pltpu.VMEM((8, N, N), F32), pltpu.VMEM((4, N, N), F32),
-            pltpu.VMEM((16 * N, N), F32), pltpu.VMEM((N, N, LANES), F32), pltpu.VMEM((N, N, LANES), F32),
-            pltpu.VMEM((16 * N, 2 * N), F32),
-            pltpu.SemaphoreType.DMA((COPIES,)), pltpu.SemaphoreType.DMA((COPIES,)), pltpu.SemaphoreType.DMA((8,)),
-            pltpu.SemaphoreType.DMA((16,)),
+            pltpu.VMEM((16 * N, N), F32), lanes, lanes, pltpu.VMEM((16 * N, 2 * N), F32),
+            pltpu.SemaphoreType.DMA((COPIES,)), pltpu.SemaphoreType.DMA((COPIES,)), pltpu.SemaphoreType.DMA((11,)),
+            pltpu.SemaphoreType.DMA((18,)),
         ],
         compiler_params=pltpu.CompilerParams(collective_id=0, has_side_effects=True, vmem_limit_bytes=VMEM),
-    )(gm, pack, tpack, it, up)
-
-
-def project(table_ref, count_ref, pos_ref, c_ref, u_hbm, t_hbm, head_hbm, inner_out, out_ref,
+    )(basis, lt, it, up)
+
+
+def project(table_ref, count_ref, c_ref, u_hbm, t_hbm, head_hbm, orth_hbm, leaf_hbm, upper_hbm,
+            inner_out, out_ref, orth_out, leaf_out, upper_out, orth_ref, leaf_ref, upper_ref,
             buf, s, r, cols, rows, all_u, all_t, inner_ref, fetch_sem, store_sem):
     fetches = []
     for q in range(4):
@@ -379,6 +372,9 @@
     fetches.append(pltpu.make_async_copy(u_hbm, all_u, fetch_sem.at[4]))
     fetches.append(pltpu.make_async_copy(t_hbm, all_t, fetch_sem.at[5]))
     fetches.append(pltpu.make_async_copy(head_hbm, inner_ref.at[pl.ds(0, 7)], fetch_sem.at[6]))
+    through = ((orth_hbm, orth_ref, orth_out), (leaf_hbm, leaf_ref, leaf_out), (upper_hbm, upper_ref, upper_out))
+    for i, (x, y, _) in enumerate(through):
+        fetches.append(pltpu.make_async_copy(x, y, fetch_sem.at[7 + i]))
     for c in fetches:
         c.start()
     lane = lax.broadcasted_iota(jnp.int32, (N, 2 * N), 1)
@@ -417,7 +413,11 @@
                 at += 1
     stores = [pltpu.make_async_copy(inner_ref, inner_out, store_sem.at[4])]
     stores[0].start()
-    base = pos_ref[0] * 64
+    for i, (_, y, z) in enumerate(through):
+        fetches[7 + i].wait()
+        stores.append(pltpu.make_async_copy(y, z, store_sem.at[5 + i]))
+        stores[-1].start()
+    base = lax.axis_index("leaf") * 64
 
     def slot(k, d):
         i = jnp.clip(table_ref[0, k] - base, 0, 63)
@@ -454,32 +454,31 @@
         c.wait()
 
 
-def run_project(pairs, counts, pos, coupling, u, t, head):
+def run_project(pairs, counts, coupling, u, t, head, orth, new_leaf, upper):
     sm = pl.BlockSpec(memory_space=pltpu.SMEM)
     hbm = pl.BlockSpec(memory_space=pl.ANY)
     sd = jax.ShapeDtypeStruct
-    inner, out = pl.pallas_call(
+    leaves = pltpu.VMEM((16, N, N), F32)
+    inner, out, orth, new_leaf, upper = pl.pallas_call(
         project,
-        out_shape=(sd((63, N, N), F32), sd((N, N, 256), F32)),
-        in_specs=[sm, sm, sm, hbm, hbm, hbm, hbm],
-        out_specs=(hbm, hbm),
+        out_shape=(sd((63, N, N), F32), sd((N, N, 256), F32), sd((16, N, N), F32), sd((16, N, N), F32), sd((1, N, N), F32)),
+        in_specs=[sm, sm] + [hbm] * 7,
+        out_specs=(hbm,) * 5,
         scratch_shapes=[
+            leaves, leaves, pltpu.VMEM((1, N, N), F32),
             pltpu.VMEM((N, N, 256), F32), pltpu.VMEM((128 * N, 2 * N), F32), pltpu.VMEM((128 * N, 2 * N), F32),
             pltpu.VMEM((192, N, 4 * N), BF), pltpu.VMEM((64, N, 2 * N), BF),
             pltpu.VMEM((96, N, 2 * N), F32), pltpu.VMEM((4, 7, N, 2 * N), F32), pltpu.VMEM((63, N, N), F32),
-            pltpu.SemaphoreType.DMA((7,)), pltpu.SemaphoreType.DMA((5,)),
+            pltpu.SemaphoreType.DMA((10,)), pltpu.SemaphoreType.DMA((8,)),
         ],
         compiler_params=pltpu.CompilerParams(vmem_limit_bytes=VMEM),
-    )(pairs.T, counts, pos, jnp.transpose(coupling, (1, 2, 0)), u, t, head)
-    return inner, jnp.transpose(out, (2, 0, 1))
+    )(pairs.T, counts, jnp.transpose(coupling, (1, 2, 0)), u, t, head, orth, new_leaf, upper)
+    return orth, new_leaf, inner, upper, jnp.transpose(out, (2, 0, 1))
 
 
 def body(leaf_basis, leaf_transfer, inner_transfer, upper_transfer, coupling, pairs, counts):
-    pos = jnp.stack([lax.axis_index("leaf"), lax.axis_index("blk")]).astype(jnp.int32)
-    gm, pack, tpack, orth, new_leaf = run_lower(pos, leaf_basis, leaf_transfer, inner_transfer)
-    all_u, all_t, head, upper = run_middle(gm, pack, tpack, inner_transfer, upper_transfer)
-    inner, out = run_project(pairs, counts, pos, coupling, all_u, all_t, head)
-    return orth, new_leaf, inner, upper, out
+    orth, new_leaf, all_u, all_t, head, upper = run_tree(leaf_basis, leaf_transfer, inner_transfer, upper_transfer)
+    return run_project(pairs, counts, coupling, all_u, all_t, head, orth, new_leaf, upper)
 
 
 def solution(mesh):

time: 84.2 us -> 74.4 us (0.88)
  Pallas kernels: 81.5 us -> 72.8 us
    pallas_call x2 -> x1, Pallas kernels: 63.4 us -> 54.6 us  [run_tree(): pl.pallas_call(tree, out_shape=(sd((16, N, N), F32), sd((16, N, N), F32),...]
where the time goes in v5:
time: 74.4 us; the launch traced here: 74.2 us
  Pallas kernels  72.8 us (98%)
  between operations  1.47 us (2%)
    pallas_call x1, Pallas kernels, run_tree(): pl.pallas_call(tree, out_shape=(sd((16, N, N), F32), sd((16, N, N), F32),...  54.6 us
    pallas_call x1, Pallas kernels, run_project(): pl.pallas_call(project, out_shape=(sd((63, N, N), F32), sd((N, N, 256), F...  18.1 us

profile of v5, /device:TPU:1, one launch (start us, length us, event | category | flops | bytes accessed | tf_op | source)
XLA Modules:
  0.0 74.2 jit_solution(2757565137776032356)
XLA Ops:
  1.3 54.6 %shard_map.110 = (f32[16,64,64]{2,1,0:T(8,128)}, f32[16,64,64]{2,1,0:T(8,128)}, f32[96,64,128]{2,1,0:T(8,128)}, f32[4,7,64,128]{3,2,1,0:T(8,128)}, f32[7,64,64]{2,1,0:T(8,128)}, /*index=5*/f32[1,64,64]{2,1,0:T(8,128)}) custom-call(f32[16,64,64]{2,1,0:T(8,128)} %basis_hbm.1, f32[16,64,64]{2,1,0:T(8,128)} %lt_hbm.1, f32[63,64,64]{2,1,0:T(8,128)} %it_hbm.1, ...), custom_call_target="tpu_custom_call" | custom-call | tf_op jit(solution)/shard_map/pallas_call | solution.py:344
  55.9 18.1 %shard_map.111 = (f32[63,64,64]{2,1,0:T(8,128)}, f32[64,64,256]{2,1,0:T(8,128)}, f32[16,64,64]{2,1,0:T(8,128)}, f32[16,64,64]{2,1,0:T(8,128)}, f32[1,64,64]{2,1,0:T(8,128)}) custom-call(s32[2,256]{1,0:T(2,128)} %bitcast.4, s32[1]{0:T(128)S(6)} %copy.12.count_ref, f32[64,64,256]{2,1,0:T(8,128)} %bitcast.3, f32[96,64,128]{2,1,0:T(8,128)} %get-tuple-element.16.u_hbm, ...), custom_call_target="tpu_custom_call" | custom-call | tf_op jit(solution)/shard_map/pallas_call | solution.py:462

commit v6 on v5

--- a/solution.py
+++ b/solution.py
@@ -135,9 +135,9 @@
     return h, l, pltpu.roll(h, N, 1), pltpu.roll(l, N, 1)
 
 
-def tree(basis_hbm, lt_hbm, it_hbm, up_hbm, orth_out, newleaf_out, u_out, t_out, head_ref, upper_ref,
-         basis_ref, lt_ref, e, tmp, orth_ref, newleaf_ref, gram_low, uw_low, pack_ref, tpack_ref, it_ref, near_up, far_up, own_up, all_u, all_t, quad, octet, four, gram, a, winv, uw,
-           send_sem, recv_sem, fetch_sem, store_sem):
+def tree(table_ref, count_ref, basis_hbm, lt_hbm, it_hbm, up_hbm, c_hbm, orth_out, newleaf_out, t_out, gram, out_ref,
+         buf, s, r, cols, rows, basis_ref, lt_ref, e, tmp, orth_ref, newleaf_ref, gram_low, uw_low, pack_ref, tpack_ref, it_ref, near_up, far_up, all_u, all_t, quad, octet, four, a, winv,
+           send_sem, recv_sem, fetch_sem, store_sem, own_sem):
     leaf, blk = lax.axis_index("leaf"), lax.axis_index("blk")
     low, high = leaf % 8, leaf // 8
     zup, zdown, zfar = [{"leaf": leaf, "blk": (blk + i) % 4} for i in (1, 3, 2)]
@@ -154,9 +154,9 @@
     for count, at in ((8, 0), (4, 8), (2, 12), (1, 14)):
         wanted.append(("e%d" % count, it_hbm.at[pl.ds(4 * count - 1 + count * blk, count)], e.at[pl.ds(at, count)]))
     wanted += [
-        ("it", it_hbm.at[pl.ds(0, 7)], it_ref), ("own", up_hbm.at[pl.ds(jnp.maximum(leaf - 1, 0), 1)], own_up),
+        ("it", it_hbm.at[pl.ds(0, 3)], it_ref),
         ("near", up_hbm.at[pl.ds(high * 8, 7)], near_up), ("far0", up_hbm.at[pl.ds(7, 1)], far_up.at[pl.ds(0, 1)]),
-        ("far1", up_hbm.at[pl.ds(23, 1)], far_up.at[pl.ds(1, 1)])]
+        ("far1", up_hbm.at[pl.ds(23, 1)], far_up.at[pl.ds(1, 1)]), ("c", c_hbm, buf)]
     for i, (name, x, y) in enumerate(wanted):
         fetches[name] = pltpu.make_async_copy(x, y, fetch_sem.at[i])
         fetches[name].start()
@@ -233,11 +233,11 @@
 
     for c in range(8):
         pack_ref[c] = jnp.concatenate([u_low(2 * c), u_low(2 * c + 1)], axis=1)
+    own_u = pltpu.make_async_copy(pack_ref, block(1, blk), own_sem.at[0])
+    own_u.start()
     u_up = push(pack_ref, block(1, blk), zup)
     u_down = push(pack_ref, block(1, blk), zdown)
     sides = [(push(pack_ref, block(0, blk), right), 0, blk), (push(pack_ref, block(2, blk), left), 2, blk)]
-    store(pack_ref, u_out.at[pl.ds((4 + blk) * 8, 8)])
-
     for c in range(16):
         orth_ref[c] = nt(basis_ref[c], w_low(c))
     store(orth_ref, orth_out)
@@ -248,7 +248,61 @@
         newleaf_ref[2 * c + 1] = x[N:]
     store(newleaf_ref, newleaf_out)
 
-    for name in ("near", "far0", "far1", "own"):
+    lane = lax.broadcasted_iota(jnp.int32, (N, 2 * N), 1)
+    lower_lanes = lane < N
+
+    def turn(k, _):
+        x = jnp.concatenate([buf[k, :, 0:128], buf[k, :, 128:256]], axis=0)
+        s[pl.ds(k, 128, stride=N), :] = x.T
+        return 0
+    fetches["c"].wait()
+    lax.fori_loop(0, N, turn, 0, unroll=8)
+
+    at, pair = 16, 0
+    for count in (8, 4, 2):
+        for n in range(0, count, 2):
+            x = jnp.concatenate([nn(u_low(at + n), e[at + n - 16]), nn(u_low(at + n + 1), e[at + n - 15])], axis=0)
+            x = nt(x, w_low(at + count + n // 2))
+            tpack_ref[pair] = jnp.concatenate([x[:N], x[N:]], axis=1)
+            pair += 1
+        at += count
+    store(tpack_ref, t_out.at[blk])
+
+    below, above, beyond = (blk + 3) % 4, (blk + 1) % 4, (blk + 2) % 4
+
+    def forward(b):
+        sides.extend([(push(block(1, b), block(0, b), right), 0, b), (push(block(1, b), block(2, b), left), 2, b)])
+
+    def prepare(p, _):
+        h, l, hr, lr = cut(all_u[p])
+        cols[2 * p] = jnp.concatenate([jnp.where(lower_lanes, h, hr), jnp.where(lower_lanes, l, lr)], axis=1).astype(BF)
+        cols[2 * p + 1] = jnp.concatenate([jnp.where(lower_lanes, hr, h), jnp.where(lower_lanes, lr, l)], axis=1).astype(BF)
+        return 0
+
+    def prepare_rows(p, _):
+        h, l, hr, lr = cut(all_u[32 + p])
+        rows[2 * p] = jnp.where(lower_lanes, h, lr).astype(BF)
+        rows[2 * p + 1] = jnp.where(lower_lanes, hr, l).astype(BF)
+        return 0
+    def split_block(d, b):
+        first = (d * 4 + b) * 8
+        if d == 1:
+            lax.fori_loop(0, 8, lambda p, _: prepare_rows(b * 8 + p, _), 0, unroll=8)
+        lax.fori_loop(0, 8, lambda p, _: prepare(first + p, _), 0, unroll=8)
+
+    u_up.wait_recv()
+    half_up = push(block(1, below, 0, 4), block(1, below, 0, 4), zup)
+    u_down.wait_recv()
+    half_down = push(block(1, above, 4, 4), block(1, above, 4, 4), zdown)
+    forward(below)
+    forward(above)
+    t_up = push(tpack_ref, all_t.at[blk], zup)
+    t_down = push(tpack_ref, all_t.at[blk], zdown)
+    own_u.wait()
+    for b in (blk, below, above):
+        split_block(1, b)
+
+    for name in ("near", "far0", "far1"):
         fetches[name].wait()
     for c in octets:
         c.wait_recv()
@@ -263,161 +317,21 @@
     four[high] = sandwich(near_up[3], third)
     fours = [push(four.at[high], four.at[high], peer) for peer in far]
 
-    below, above, beyond = (blk + 3) % 4, (blk + 1) % 4, (blk + 2) % 4
-    u_up.wait_recv()
-    half_up = push(block(1, below, 0, 4), block(1, below, 0, 4), zup)
-    u_down.wait_recv()
-    half_down = push(block(1, above, 4, 4), block(1, above, 4, 4), zdown)
-    for b in (below, above):
-        sides += [(push(block(1, b), block(0, b), right), 0, b), (push(block(1, b), block(2, b), left), 2, b)]
-        store(block(1, b), u_out.at[pl.ds((4 + b) * 8, 8)])
-
-    at, pair = 16, 0
-    for count in (8, 4, 2):
-        for n in range(0, count, 2):
-            x = jnp.concatenate([nn(u_low(at + n), e[at + n - 16]), nn(u_low(at + n + 1), e[at + n - 15])], axis=0)
-            x = nt(x, w_low(at + count + n // 2))
-            tpack_ref[pair] = jnp.concatenate([x[:N], x[N:]], axis=1)
-            pair += 1
-        at += count
-    store(tpack_ref, t_out.at[blk])
-    t_up = push(tpack_ref, all_t.at[blk], zup)
-    t_down = push(tpack_ref, all_t.at[blk], zdown)
-
-    for c in fours:
-        c.wait_recv()
-    fourth = [four[2 * n] + four[2 * n + 1] for n in range(2)]
-    keep(10, jnp.where(high < 2, fourth[0], fourth[1]))
-    images = [sandwich(far_up[n], fourth[n]) for n in range(2)]
-    for n in range(11, 16):
-        keep(n, images[0] + images[1])
-
-    def opposite():
-        half_up.wait_recv()
-        half_down.wait_recv()
-        sides.extend([(push(block(1, beyond), block(0, beyond), right), 0, beyond), (push(block(1, beyond), block(2, beyond), left), 2, beyond)])
-        store(block(1, beyond), u_out.at[pl.ds((4 + beyond) * 8, 8)])
-
-    factor_stack(gram, uw, a, winv, 16, loaded=opposite)
-
+    half_up.wait_recv()
+    half_down.wait_recv()
+    forward(beyond)
+    split_block(1, beyond)
     t_up.wait_recv()
     t_half_up = push(all_t.at[below, pl.ds(0, 4)], all_t.at[below, pl.ds(0, 4)], zup)
     t_down.wait_recv()
     t_half_down = push(all_t.at[above, pl.ds(4, 3)], all_t.at[above, pl.ds(4, 3)], zdown)
     for b in (below, above):
         store(all_t.at[b], t_out.at[b])
-
-    def u(i):
-        return uw[pl.ds(i * N, N), 0:N]
-
-    def w(i):
-        return uw[pl.ds(i * N, N), N:2 * N]
-
-    head_ref[0] = nt(nn(u(6), it_ref[0]), w(7))
-    for n in range(2):
-        head_ref[1 + n] = nt(nn(u(4 + n), it_ref[1 + n]), w(6))
-    for n in range(4):
-        head_ref[3 + n] = nt(nn(u(n), it_ref[3 + n]), w(4 + n // 2))
-    level = jnp.where(leaf % 2 == 1, 1, jnp.where(leaf % 4 == 2, 2, jnp.where(leaf % 8 == 4, 3, jnp.where(leaf % 16 == 8, 4, 5))))
-    carried = nn(u(6 + level), own_up[0])
-    renewed = nt(carried, w(jnp.minimum(7 + level, 11)))
-    upper_ref[0] = jnp.where(leaf == 0, u(11), jnp.where(leaf == 16, carried, renewed))
-
     for c, d, b in sides:
         c.wait_recv()
-        store(block(d, b), u_out.at[pl.ds((d * 4 + b) * 8, 8)])
-    t_half_up.wait_recv()
-    t_half_down.wait_recv()
-    store(all_t.at[beyond], t_out.at[beyond])
-    for c in used:
-        c.wait_send()
-    for c in stores:
-        c.wait()
-
-
-def run_tree(basis, lt, it, up):
-    vm = pl.BlockSpec(memory_space=pltpu.VMEM)
-    hbm = pl.BlockSpec(memory_space=pl.ANY)
-    sd = jax.ShapeDtypeStruct
-    leaves = pltpu.VMEM((16, N, N), F32)
-    lanes = pltpu.VMEM((N, N, LANES), F32)
-    return pl.pallas_call(
-        tree,
-        out_shape=(sd((16, N, N), F32), sd((16, N, N), F32), sd((96, N, 2 * N), F32), sd((4, 7, N, 2 * N), F32),
-                   sd((7, N, N), F32), sd((1, N, N), F32)),
-        in_specs=[hbm] * 4,
-        out_specs=(hbm, hbm, hbm, hbm, vm, vm),
-        scratch_shapes=[
-            leaves, leaves, pltpu.VMEM((15, N, N), F32), pltpu.VMEM((32, N, N), F32), leaves, leaves,
-            pltpu.VMEM((32 * N, N), F32), pltpu.VMEM((32 * N, 2 * N), F32),
-            pltpu.VMEM((8, N, 2 * N), F32), pltpu.VMEM((7, N, 2 * N), F32), pltpu.VMEM((7, N, N), F32),
-            pltpu.VMEM((7, N, N), F32), pltpu.VMEM((2, N, N), F32), pltpu.VMEM((1, N, N), F32),
-            pltpu.VMEM((96, N, 2 * N), F32), pltpu.VMEM((4, 7, N, 2 * N), F32),
-            pltpu.VMEM((4, N, 2 * N), F32), pltpu.VMEM((8, N, N), F32), pltpu.VMEM((4, N, N), F32),
-            pltpu.VMEM((16 * N, N), F32), lanes, lanes, pltpu.VMEM((16 * N, 2 * N), F32),
-            pltpu.SemaphoreType.DMA((COPIES,)), pltpu.SemaphoreType.DMA((COPIES,)), pltpu.SemaphoreType.DMA((11,)),
-            pltpu.SemaphoreType.DMA((18,)),
-        ],
-        compiler_params=pltpu.CompilerParams(collective_id=0, has_side_effects=True, vmem_limit_bytes=VMEM),
-    )(basis, lt, it, up)
-
-
-def project(table_ref, count_ref, c_ref, u_hbm, t_hbm, head_hbm, orth_hbm, leaf_hbm, upper_hbm,
-            inner_out, out_ref, orth_out, leaf_out, upper_out, orth_ref, leaf_ref, upper_ref,
-            buf, s, r, cols, rows, all_u, all_t, inner_ref, fetch_sem, store_sem):
-    fetches = []
-    for q in range(4):
-        part = pl.ds(16 * q, 16)
-        fetches.append(pltpu.make_async_copy(c_ref.at[part], buf.at[part], fetch_sem.at[q]))
-    fetches.append(pltpu.make_async_copy(u_hbm, all_u, fetch_sem.at[4]))
-    fetches.append(pltpu.make_async_copy(t_hbm, all_t, fetch_sem.at[5]))
-    fetches.append(pltpu.make_async_copy(head_hbm, inner_ref.at[pl.ds(0, 7)], fetch_sem.at[6]))
-    through = ((orth_hbm, orth_ref, orth_out), (leaf_hbm, leaf_ref, leaf_out), (upper_hbm, upper_ref, upper_out))
-    for i, (x, y, _) in enumerate(through):
-        fetches.append(pltpu.make_async_copy(x, y, fetch_sem.at[7 + i]))
-    for c in fetches:
-        c.start()
-    lane = lax.broadcasted_iota(jnp.int32, (N, 2 * N), 1)
-    lower_lanes = lane < N
-
-    def turn(k, _):
-        x = jnp.concatenate([buf[k, :, 0:128], buf[k, :, 128:256]], axis=0)
-        s[pl.ds(k, 128, stride=N), :] = x.T
-        return 0
-    for q in range(4):
-        fetches[q].wait()
-        lax.fori_loop(16 * q, 16 * q + 16, turn, 0, unroll=8)
-
-    def prepare(p, _):
-        h, l, hr, lr = cut(all_u[p])
-        cols[2 * p] = jnp.concatenate([jnp.where(lower_lanes, h, hr), jnp.where(lower_lanes, l, lr)], axis=1).astype(BF)
-        cols[2 * p + 1] = jnp.concatenate([jnp.where(lower_lanes, hr, h), jnp.where(lower_lanes, lr, l)], axis=1).astype(BF)
-        return 0
-
-    def prepare_rows(p, _):
-        h, l, hr, lr = cut(all_u[32 + p])
-        rows[2 * p] = jnp.where(lower_lanes, h, lr).astype(BF)
-        rows[2 * p + 1] = jnp.where(lower_lanes, hr, l).astype(BF)
-        return 0
-    fetches[4].wait()
-    lax.fori_loop(0, 96, prepare, 0, unroll=8)
-    lax.fori_loop(0, 32, prepare_rows, 0, unroll=8)
-
-    fetches[5].wait()
-    fetches[6].wait()
-    for b in range(4):
-        at = 0
-        for count in (8, 4, 2):
-            for n in range(count):
-                inner_ref[4 * count - 1 + count * b + n] = all_t[b, at // 2, :, at % 2 * N:at % 2 * N + N]
-                at += 1
-    stores = [pltpu.make_async_copy(inner_ref, inner_out, store_sem.at[4])]
-    stores[0].start()
-    for i, (_, y, z) in enumerate(through):
-        fetches[7 + i].wait()
-        stores.append(pltpu.make_async_copy(y, z, store_sem.at[5 + i]))
-        stores[-1].start()
-    base = lax.axis_index("leaf") * 64
+        split_block(d, b)
+
+    base = leaf * 64
 
     def slot(k, d):
         i = jnp.clip(table_ref[0, k] - base, 0, 63)
@@ -437,6 +351,14 @@
         return 0
     lax.fori_loop(0, 128, both, 0, unroll=32)
 
+    for c in fours:
+        c.wait_recv()
+    fourth = [four[2 * n] + four[2 * n + 1] for n in range(2)]
+    keep(10, jnp.where(high < 2, fourth[0], fourth[1]))
+    images = [sandwich(far_up[n], fourth[n]) for n in range(2)]
+    for n in range(11, 16):
+        keep(n, images[0] + images[1])
+
     live = count_ref[0]
 
     def back(k, _):
@@ -447,38 +369,127 @@
     for q in range(4):
         lax.fori_loop(16 * q, 16 * q + 16, back, 0, unroll=8)
         part = pl.ds(16 * q, 16)
-        c = pltpu.make_async_copy(buf.at[part], out_ref.at[part], store_sem.at[q])
-        c.start()
-        stores.append(c)
+        store(buf.at[part], out_ref.at[part])
+
+    t_half_up.wait_recv()
+    t_half_down.wait_recv()
+    store(all_t.at[beyond], t_out.at[beyond])
+    for c in used:
+        c.wait_send()
     for c in stores:
         c.wait()
 
 
-def run_project(pairs, counts, coupling, u, t, head, orth, new_leaf, upper):
+def run_tree(pairs, counts, basis, lt, it, up, coupling):
+    vm = pl.BlockSpec(memory_space=pltpu.VMEM)
     sm = pl.BlockSpec(memory_space=pltpu.SMEM)
     hbm = pl.BlockSpec(memory_space=pl.ANY)
     sd = jax.ShapeDtypeStruct
     leaves = pltpu.VMEM((16, N, N), F32)
-    inner, out, orth, new_leaf, upper = pl.pallas_call(
-        project,
-        out_shape=(sd((63, N, N), F32), sd((N, N, 256), F32), sd((16, N, N), F32), sd((16, N, N), F32), sd((1, N, N), F32)),
-        in_specs=[sm, sm] + [hbm] * 7,
+    lanes = pltpu.VMEM((N, N, LANES), F32)
+    return pl.pallas_call(
+        tree,
+        out_shape=(sd((16, N, N), F32), sd((16, N, N), F32), sd((4, 7, N, 2 * N), F32), sd((16 * N, N), F32), sd((N, N, 256), F32)),
+        in_specs=[sm, sm] + [hbm] * 5,
+        out_specs=(hbm, hbm, hbm, vm, hbm),
+        scratch_shapes=[
+            pltpu.VMEM((N, N, 256), F32), pltpu.VMEM((128 * N, 2 * N), F32), pltpu.VMEM((128 * N, 2 * N), F32),
+            pltpu.VMEM((192, N, 4 * N), BF), pltpu.VMEM((64, N, 2 * N), BF),
+            leaves, leaves, pltpu.VMEM((15, N, N), F32), pltpu.VMEM((32, N, N), F32), leaves, leaves,
+            pltpu.VMEM((32 * N, N), F32), pltpu.VMEM((32 * N, 2 * N), F32),
+            pltpu.VMEM((8, N, 2 * N), F32), pltpu.VMEM((7, N, 2 * N), F32), pltpu.VMEM((3, N, N), F32),
+            pltpu.VMEM((7, N, N), F32), pltpu.VMEM((2, N, N), F32),
+            pltpu.VMEM((96, N, 2 * N), F32), pltpu.VMEM((4, 7, N, 2 * N), F32),
+            pltpu.VMEM((4, N, 2 * N), F32), pltpu.VMEM((8, N, N), F32), pltpu.VMEM((4, N, N), F32), lanes, lanes,
+            pltpu.SemaphoreType.DMA((COPIES,)), pltpu.SemaphoreType.DMA((COPIES,)), pltpu.SemaphoreType.DMA((11,)),
+            pltpu.SemaphoreType.DMA((10,)), pltpu.SemaphoreType.DMA((1,)),
+        ],
+        compiler_params=pltpu.CompilerParams(collective_id=0, has_side_effects=True, vmem_limit_bytes=VMEM),
+    )(pairs.T, counts, basis, lt, it, up, jnp.transpose(coupling, (1, 2, 0)))
+
+
+def top(gram_hbm, it_hbm, up_hbm, orth_hbm, leaf_hbm, t_hbm, proj_hbm,
+        orth_out, leaf_out, inner_out, upper_out, proj_out,
+        gram, it_ref, own_up, orth_ref, leaf_ref, all_t, inner_ref, upper_ref, proj_ref, a, winv, uw, fetch_sem, store_sem):
+    leaf = lax.axis_index("leaf")
+    fetches = []
+    for i, (x, y) in enumerate((
+            (gram_hbm, gram), (t_hbm, all_t), (it_hbm.at[pl.ds(0, 7)], it_ref),
+            (up_hbm.at[pl.ds(jnp.maximum(leaf - 1, 0), 1)], own_up),
+            (orth_hbm, orth_ref), (leaf_hbm, leaf_ref), (proj_hbm, proj_ref))):
+        fetches.append(pltpu.make_async_copy(x, y, fetch_sem.at[i]))
+        fetches[-1].start()
+    stores = []
+
+    def store(src, dst):
+        stores.append(pltpu.make_async_copy(src, dst, store_sem.at[len(stores)]))
+        stores[-1].start()
+
+    def pass_through():
+        for i, (y, z) in enumerate(((orth_ref, orth_out), (leaf_ref, leaf_out), (proj_ref, proj_out))):
+            fetches[4 + i].wait()
+            store(y, z)
+        fetches[1].wait()
+        for b in range(4):
+            at = 0
+            for count in (8, 4, 2):
+                for n in range(count):
+                    inner_ref[4 * count - 1 + count * b + n] = all_t[b, at // 2, :, at % 2 * N:at % 2 * N + N]
+                    at += 1
+        store(inner_ref.at[pl.ds(7, 56)], inner_out.at[pl.ds(7, 56)])
+
+    fetches[0].wait()
+    factor_stack(gram, uw, a, winv, 16, eliminated=pass_through)
+    for i in (2, 3):
+        fetches[i].wait()
+
+    def u(i):
+        return uw[pl.ds(i * N, N), 0:N]
+
+    def w(i):
+        return uw[pl.ds(i * N, N), N:2 * N]
+
+    inner_ref[0] = nt(nn(u(6), it_ref[0]), w(7))
+    for n in range(2):
+        inner_ref[1 + n] = nt(nn(u(4 + n), it_ref[1 + n]), w(6))
+    for n in range(4):
+        inner_ref[3 + n] = nt(nn(u(n), it_ref[3 + n]), w(4 + n // 2))
+    store(inner_ref.at[pl.ds(0, 7)], inner_out.at[pl.ds(0, 7)])
+    level = jnp.where(leaf % 2 == 1, 1, jnp.where(leaf % 4 == 2, 2, jnp.where(leaf % 8 == 4, 3, jnp.where(leaf % 16 == 8, 4, 5))))
+    carried = nn(u(6 + level), own_up[0])
+    renewed = nt(carried, w(jnp.minimum(7 + level, 11)))
+    upper_ref[0] = jnp.where(leaf == 0, u(11), jnp.where(leaf == 16, carried, renewed))
+    store(upper_ref, upper_out)
+    for c in stores:
+        c.wait()
+
+
+def run_top(gram, it, up, orth, new_leaf, t, proj):
+    hbm = pl.BlockSpec(memory_space=pl.ANY)
+    sd = jax.ShapeDtypeStruct
+    leaves = pltpu.VMEM((16, N, N), F32)
+    one = pltpu.VMEM((1, N, N), F32)
+    lanes = pltpu.VMEM((N, N, LANES), F32)
+    return pl.pallas_call(
+        top,
+        out_shape=(sd((16, N, N), F32), sd((16, N, N), F32), sd((63, N, N), F32), sd((1, N, N), F32), sd((N, N, 256), F32)),
+        in_specs=[hbm] * 7,
         out_specs=(hbm,) * 5,
         scratch_shapes=[
-            leaves, leaves, pltpu.VMEM((1, N, N), F32),
-            pltpu.VMEM((N, N, 256), F32), pltpu.VMEM((128 * N, 2 * N), F32), pltpu.VMEM((128 * N, 2 * N), F32),
-            pltpu.VMEM((192, N, 4 * N), BF), pltpu.VMEM((64, N, 2 * N), BF),
-            pltpu.VMEM((96, N, 2 * N), F32), pltpu.VMEM((4, 7, N, 2 * N), F32), pltpu.VMEM((63, N, N), F32),
-            pltpu.SemaphoreType.DMA((10,)), pltpu.SemaphoreType.DMA((8,)),
+            pltpu.VMEM((16 * N, N), F32), pltpu.VMEM((7, N, N), F32), one, leaves, leaves,
+            pltpu.VMEM((4, 7, N, 2 * N), F32), pltpu.VMEM((63, N, N), F32), one, pltpu.VMEM((N, N, 256), F32),
+            lanes, lanes, pltpu.VMEM((16 * N, 2 * N), F32),
+            pltpu.SemaphoreType.DMA((7,)), pltpu.SemaphoreType.DMA((6,)),
         ],
         compiler_params=pltpu.CompilerParams(vmem_limit_bytes=VMEM),
-    )(pairs.T, counts, jnp.transpose(coupling, (1, 2, 0)), u, t, head, orth, new_leaf, upper)
-    return orth, new_leaf, inner, upper, jnp.transpose(out, (2, 0, 1))
+    )(gram, it, up, orth, new_leaf, t, proj)
 
 
 def body(leaf_basis, leaf_transfer, inner_transfer, upper_transfer, coupling, pairs, counts):
-    orth, new_leaf, all_u, all_t, head, upper = run_tree(leaf_basis, leaf_transfer, inner_transfer, upper_transfer)
-    return run_project(pairs, counts, coupling, all_u, all_t, head, orth, new_leaf, upper)
+    orth, new_leaf, all_t, gram, proj = run_tree(
+        pairs, counts, leaf_basis, leaf_transfer, inner_transfer, upper_transfer, coupling)
+    orth, new_leaf, inner, upper, proj = run_top(gram, inner_transfer, upper_transfer, orth, new_leaf, all_t, proj)
+    return orth, new_leaf, inner, upper, jnp.transpose(proj, (2, 0, 1))
 
 
 def solution(mesh):

time: 74.4 us -> 66.5 us (0.89)
  the two profiles are of different devices: /device:TPU:1 before, /device:TPU:0 now
where the time goes in v6:
time: 66.5 us; the launch traced here: 66.3 us
  Pallas kernels  64.8 us (97%)
  between operations  1.47 us (2%)
    pallas_call x1, Pallas kernels, run_tree(): pl.pallas_call(tree, out_shape=(sd((16, N, N), F32), sd((16, N, N), F32),...  53.8 us
    pallas_call x1, Pallas kernels, run_top(): pl.pallas_call(top, out_shape=(sd((16, N, N), F32), sd((16, N, N), F32),...  11.1 us

profile of v6, /device:TPU:0, one launch (start us, length us, event | category | flops | bytes accessed | tf_op | source)
XLA Modules:
  0.0 66.3 jit_solution(10283541161318528604)
XLA Ops:
  1.3 53.8 %shard_map.110 = (f32[16,64,64]{2,1,0:T(8,128)}, f32[16,64,64]{2,1,0:T(8,128)}, f32[4,7,64,128]{3,2,1,0:T(8,128)}, f32[1024,64]{1,0:T(8,128)}, f32[64,64,256]{2,1,0:T(8,128)}) custom-call(s32[2,256]{1,0:T(2,128)} %bitcast.4, s32[1]{0:T(128)S(6)} %copy.12.count_ref, f32[16,64,64]{2,1,0:T(8,128)} %basis_hbm.1, f32[16,64,64]{2,1,0:T(8,128)} %lt_hbm.1, ...), custom_call_target="tpu_custom_call" | custom-call | tf_op jit(solution)/shard_map/pallas_call | solution.py:390
  55.1 11.1 %shard_map.111 = (f32[16,64,64]{2,1,0:T(8,128)}, f32[16,64,64]{2,1,0:T(8,128)}, f32[63,64,64]{2,1,0:T(8,128)}, f32[1,64,64]{2,1,0:T(8,128)}, f32[64,64,256]{2,1,0:T(8,128)}) custom-call(f32[1024,64]{1,0:T(8,128)} %get-tuple-element.15.gram_hbm, f32[63,64,64]{2,1,0:T(8,128)} %it_hbm.3, f32[31,64,64]{2,1,0:T(8,128)} %up_hbm.3, ...), custom_call_target="tpu_custom_call" | custom-call | tf_op jit(solution)/shard_map/pallas_call | solution.py:473

commit v7 on v6

--- a/solution.py
+++ b/solution.py
@@ -133,6 +133,32 @@
 def cut(x):
     h, l = split(x)
     return h, l, pltpu.roll(h, N, 1), pltpu.roll(l, N, 1)
+
+
+def halves():
+    lane = lax.broadcasted_iota(jnp.int32, (16, 2 * N), 1)
+    return jnp.where(lane < N, lane, lane - N)
+
+
+def fold(x, y):
+    col = halves()
+
+    def ends(z):
+        return jnp.where(col < 16, pltpu.roll(z[48:64], 80, 1), z[16:32])
+    return jnp.concatenate(
+        [x[0:16], ends(x), y[0:16], ends(y), jnp.where(col < 32, pltpu.roll(y[32:48], 96, 1), x[32:48])], axis=0)
+
+
+def unfold(z):
+    col = halves()
+    zero = F32(0)
+
+    def build(head, ends, third):
+        return jnp.concatenate(
+            [head, jnp.where(col < 16, zero, ends), third, pltpu.roll(jnp.where(col < 16, ends, zero), 48, 1)], axis=0)
+    shared = z[64:80]
+    return (build(z[0:16], z[16:32], jnp.where(col < 32, zero, shared)),
+            build(z[32:48], z[48:64], pltpu.roll(jnp.where(col < 32, shared, zero), 32, 1)))
 
 
 def tree(table_ref, count_ref, basis_hbm, lt_hbm, it_hbm, up_hbm, c_hbm, orth_out, newleaf_out, t_out, gram, out_ref,
@@ -176,8 +202,8 @@
         c.start()
         stores.append(c)
 
-    def block(d, b, start=0, count=8):
-        return all_u.at[pl.ds((d * 4 + b) * 8 + start, count)]
+    def block(d, b, start=0, count=4):
+        return all_u.at[pl.ds((d * 4 + b) * 4 + start, count)]
 
     def keep(i, g):
         gram[i * N:i * N + N, :] = g
@@ -231,8 +257,9 @@
     def w_low(i):
         return uw_low[i * N:i * N + N, N:2 * N]
 
-    for c in range(8):
-        pack_ref[c] = jnp.concatenate([u_low(2 * c), u_low(2 * c + 1)], axis=1)
+    for c in range(4):
+        pack_ref[c] = fold(jnp.concatenate([u_low(4 * c), u_low(4 * c + 1)], axis=1),
+                           jnp.concatenate([u_low(4 * c + 2), u_low(4 * c + 3)], axis=1))
     own_u = pltpu.make_async_copy(pack_ref, block(1, blk), own_sem.at[0])
     own_u.start()
     u_up = push(pack_ref, block(1, blk), zup)
@@ -273,27 +300,31 @@
     def forward(b):
         sides.extend([(push(block(1, b), block(0, b), right), 0, b), (push(block(1, b), block(2, b), left), 2, b)])
 
-    def prepare(p, _):
-        h, l, hr, lr = cut(all_u[p])
-        cols[2 * p] = jnp.concatenate([jnp.where(lower_lanes, h, hr), jnp.where(lower_lanes, l, lr)], axis=1).astype(BF)
-        cols[2 * p + 1] = jnp.concatenate([jnp.where(lower_lanes, hr, h), jnp.where(lower_lanes, lr, l)], axis=1).astype(BF)
-        return 0
-
-    def prepare_rows(p, _):
-        h, l, hr, lr = cut(all_u[32 + p])
-        rows[2 * p] = jnp.where(lower_lanes, h, lr).astype(BF)
-        rows[2 * p + 1] = jnp.where(lower_lanes, hr, l).astype(BF)
-        return 0
+    def prepare(q, _):
+        for t, x in enumerate(unfold(all_u[q])):
+            h, l, hr, lr = cut(x)
+            at = 4 * q + 2 * t
+            cols[at] = jnp.concatenate([jnp.where(lower_lanes, h, hr), jnp.where(lower_lanes, l, lr)], axis=1).astype(BF)
+            cols[at + 1] = jnp.concatenate([jnp.where(lower_lanes, hr, h), jnp.where(lower_lanes, lr, l)], axis=1).astype(BF)
+        return 0
+
+    def prepare_rows(q, _):
+        for t, x in enumerate(unfold(all_u[16 + q])):
+            h, l, hr, lr = cut(x)
+            rows[4 * q + 2 * t] = jnp.where(lower_lanes, h, lr).astype(BF)
+            rows[4 * q + 2 * t + 1] = jnp.where(lower_lanes, hr, l).astype(BF)
+        return 0
+
     def split_block(d, b):
-        first = (d * 4 + b) * 8
+        first = (d * 4 + b) * 4
         if d == 1:
-            lax.fori_loop(0, 8, lambda p, _: prepare_rows(b * 8 + p, _), 0, unroll=8)
-        lax.fori_loop(0, 8, lambda p, _: prepare(first + p, _), 0, unroll=8)
+            lax.fori_loop(0, 4, lambda q, _: prepare_rows(b * 4 + q, _), 0, unroll=4)
+        lax.fori_loop(0, 4, lambda q, _: prepare(first + q, _), 0, unroll=4)
 
     u_up.wait_recv()
-    half_up = push(block(1, below, 0, 4), block(1, below, 0, 4), zup)
+    half_up = push(block(1, below, 0, 2), block(1, below, 0, 2), zup)
     u_down.wait_recv()
-    half_down = push(block(1, above, 4, 4), block(1, above, 4, 4), zdown)
+    half_down = push(block(1, above, 2, 2), block(1, above, 2, 2), zdown)
     forward(below)
     forward(above)
     t_up = push(tpack_ref, all_t.at[blk], zup)
@@ -302,6 +333,10 @@
     for b in (blk, below, above):
         split_block(1, b)
 
+    half_up.wait_recv()
+    half_down.wait_recv()
+    forward(beyond)
+    split_block(1, beyond)
     for name in ("near", "far0", "far1"):
         fetches[name].wait()
     for c in octets:
@@ -317,10 +352,6 @@
     four[high] = sandwich(near_up[3], third)
     fours = [push(four.at[high], four.at[high], peer) for peer in far]
 
-    half_up.wait_recv()
-    half_down.wait_recv()
-    forward(beyond)
-    split_block(1, beyond)
     t_up.wait_recv()
     t_half_up = push(all_t.at[below, pl.ds(0, 4)], all_t.at[below, pl.ds(0, 4)], zup)
     t_down.wait_recv()
@@ -397,9 +428,9 @@
             pltpu.VMEM((192, N, 4 * N), BF), pltpu.VMEM((64, N, 2 * N), BF),
             leaves, leaves, pltpu.VMEM((15, N, N), F32), pltpu.VMEM((32, N, N), F32), leaves, leaves,
             pltpu.VMEM((32 * N, N), F32), pltpu.VMEM((32 * N, 2 * N), F32),
-            pltpu.VMEM((8, N, 2 * N), F32), pltpu.VMEM((7, N, 2 * N), F32), pltpu.VMEM((3, N, N), F32),
+            pltpu.VMEM((4, 80, 2 * N), F32), pltpu.VMEM((7, N, 2 * N), F32), pltpu.VMEM((3, N, N), F32),
             pltpu.VMEM((7, N, N), F32), pltpu.VMEM((2, N, N), F32),
-            pltpu.VMEM((96, N, 2 * N), F32), pltpu.VMEM((4, 7, N, 2 * N), F32),
+            pltpu.VMEM((48, 80, 2 * N), F32), pltpu.VMEM((4, 7, N, 2 * N), F32),
             pltpu.VMEM((4, N, 2 * N), F32), pltpu.VMEM((8, N, N), F32), pltpu.VMEM((4, N, N), F32), lanes, lanes,
             pltpu.SemaphoreType.DMA((COPIES,)), pltpu.SemaphoreType.DMA((COPIES,)), pltpu.SemaphoreType.DMA((11,)),
             pltpu.SemaphoreType.DMA((10,)), pltpu.SemaphoreType.DMA((1,)),

time: 66.5 us -> 62.8 us (0.944)
  the two profiles are of different devices: /device:TPU:0 before, /device:TPU:1 now
where the time goes in v7:
time: 62.8 us; the launch traced here: 61.9 us
  Pallas kernels  60.5 us (96%)
  between operations  1.47 us (2%)
    pallas_call x1, Pallas kernels, run_tree(): pl.pallas_call(tree, out_shape=(sd((16, N, N), F32), sd((16, N, N), F32),...  49.4 us
    pallas_call x1, Pallas kernels, run_top(): pl.pallas_call(top, out_shape=(sd((16, N, N), F32), sd((16, N, N), F32),...  11.1 us

profile of v7, /device:TPU:1, one launch (start us, length us, event | category | flops | bytes accessed | tf_op | source)
XLA Modules:
  0.0 61.9 jit_solution(9346530897097684563)
XLA Ops:
  1.3 49.4 %shard_map.110 = (f32[16,64,64]{2,1,0:T(8,128)}, f32[16,64,64]{2,1,0:T(8,128)}, f32[4,7,64,128]{3,2,1,0:T(8,128)}, f32[1024,64]{1,0:T(8,128)}, f32[64,64,256]{2,1,0:T(8,128)}) custom-call(s32[2,256]{1,0:T(2,128)} %bitcast.4, s32[1]{0:T(128)S(6)} %copy.12.count_ref, f32[16,64,64]{2,1,0:T(8,128)} %basis_hbm.1, f32[16,64,64]{2,1,0:T(8,128)} %lt_hbm.1, ...), custom_call_target="tpu_custom_call" | custom-call | tf_op jit(solution)/shard_map/pallas_call | solution.py:421
  50.7 11.1 %shard_map.111 = (f32[16,64,64]{2,1,0:T(8,128)}, f32[16,64,64]{2,1,0:T(8,128)}, f32[63,64,64]{2,1,0:T(8,128)}, f32[1,64,64]{2,1,0:T(8,128)}, f32[64,64,256]{2,1,0:T(8,128)}) custom-call(f32[1024,64]{1,0:T(8,128)} %get-tuple-element.15.gram_hbm, f32[63,64,64]{2,1,0:T(8,128)} %it_hbm.3, f32[31,64,64]{2,1,0:T(8,128)} %up_hbm.3, ...), custom_call_target="tpu_custom_call" | custom-call | tf_op jit(solution)/shard_map/pallas_call | solution.py:504
